TPU v7x, 32 devices: a whole 2x2x4 slice. The times are simulated.
32 devices in a mesh: grp: 2 (over x), row: 16 (over z, y, core).
Axes of the slice: x: 2, y: 2, z: 4, core: 2. Of those that a mesh axis runs over, the one named last changes fastest.
Arguments:
- object_slices: float32 [2, 2, 2048, 2048], P(None, None, ('grp', 'row')), parts along dimension 2
- probe_modes: float32 [8, 2, 128, 128], P('grp'), parts along dimension 0, may hold values from -2.1 to 2.1
- propagator_phase: float32 [128, 128], replicated, may hold values from -3.140625 to 3.140625
- measured: float32 [256, 128, 128], P(('grp', 'row')), parts along dimension 0, may hold values from 0.25 to 4
- offsets: int32 [256, 2], P(('grp', 'row')), parts along dimension 0, may hold values from 0 to 1920, as said below
- counts: int32 [32], P(('grp', 'row')), parts along dimension 0, may hold values from 1 to 8, 72 in all
Outputs:
- object_grad: float32 [2, 2, 2048, 2048], P(None, None, ('grp', 'row')), parts along dimension 2
- probe_step: float32 [8, 2, 128, 128], P('grp'), parts along dimension 0
There are 2 independent parts, one for each index of `grp`. A program takes and returns all parts, laid end to end along the dimension named above; an argument that names none is the same for every part. Nothing has to cross between parts.
Inputs may be any that keep to these rules, and one draw needn't show every extreme that they name: The slots of device d (slots d * 8 to d * 8 + 7) have row offsets d * 64 to d * 64 + 63 and column offsets 0 to 1920. `counts`: counts sum to 72; some device holds 8.
All inputs are finite; a program needn't handle non-finite values.
Results may differ from a plain program's by a relative error of at most 0.0003.
Values sent between devices are 32-bit elements; how exact they have to be, the bound alone decides.
No kernel may reach another device: no remote copies, remote signals or barrier semaphores. Data moves between devices by JAX's collectives and lax.ppermute only.
A program may use at most 64 MiB of HBM per device.

v0:
```python
import math

import jax
import jax.numpy as jnp
from jax import lax
from jax.sharding import PartitionSpec as P


def from_behind(array, axis, by):
    peers = lax.axis_size(axis)
    return lax.ppermute(array, axis, [(i, (i + by) % peers) for i in range(peers)])


def contract(form, first, second):
    return jnp.einsum(form, first, second, precision=lax.Precision.HIGHEST)


def fourier_tables(pixels):
    indices = jnp.arange(pixels, dtype=jnp.int32)
    phases = indices[:, None] * indices[None, :] % pixels
    angles = phases.astype(jnp.float32) * (2.0 * math.pi / pixels)
    scale_factor = 1.0 / math.sqrt(pixels)
    return (jnp.cos(angles) * scale_factor, -jnp.sin(angles) * scale_factor)


def transform(table_re, table_im, real_part, imag_part):
    left_re = contract("ij,mjk->mik", table_re, real_part) - contract(
        "ij,mjk->mik", table_im, imag_part
    )
    left_im = contract("ij,mjk->mik", table_re, imag_part) + contract(
        "ij,mjk->mik", table_im, real_part
    )
    right_re = contract("mij,jk->mik", left_re, table_re) - contract(
        "mij,jk->mik", left_im, table_im
    )
    right_im = contract("mij,jk->mik", left_re, table_im) + contract(
        "mij,jk->mik", left_im, table_re
    )
    return (right_re, right_im)


def propagate(table_re, table_im, wave_re, wave_im, prop_re, prop_im):
    far_re, far_im = transform(table_re, table_im, wave_re, wave_im)
    turned_re = far_re * prop_re - far_im * prop_im
    turned_im = far_re * prop_im + far_im * prop_re
    return transform(table_re, -table_im, turned_re, turned_im)


def patch_loss(patches, probe_modes, target, table_re, table_im, prop_re, prop_im):
    wave_re = probe_modes[:, 0]
    wave_im = probe_modes[:, 1]
    for layer_index in range(patches.shape[0]):
        if layer_index > 0:
            wave_re, wave_im = propagate(table_re, table_im, wave_re, wave_im, prop_re, prop_im)
        trans_re = patches[layer_index, 0]
        trans_im = patches[layer_index, 1]
        wave_re, wave_im = (
            wave_re * trans_re - wave_im * trans_im,
            wave_re * trans_im + wave_im * trans_re,
        )
    far_re, far_im = transform(table_re, table_im, wave_re, wave_im)
    intensity = jnp.sum(far_re * far_re + far_im * far_im, axis=0)
    misfit = intensity - target
    return 0.5 * jnp.sum(misfit * misfit)


def local(object_slices, probe_modes, propagator_phase, measured, offsets, counts):
    slices = object_slices.shape[0]
    tile_rows = object_slices.shape[2]
    pixels = probe_modes.shape[-1]
    table_re, table_im = fourier_tables(pixels)
    prop_re = jnp.cos(propagator_phase)
    prop_im = jnp.sin(propagator_phase)
    first_row = lax.axis_index("row") * tile_rows
    anchor = jnp.zeros((), jnp.int32)

    def slot_terms(patches, slot_index):
        target = lax.dynamic_index_in_dim(measured, slot_index, 0, keepdims=False)

        def local_loss(patch_part, probe_part):
            return patch_loss(patch_part, probe_part, target, table_re, table_im, prop_re, prop_im)

        misfit_sum, pullback = jax.vjp(local_loss, patches, probe_modes)
        patch_grad, probe_part = pullback(jnp.ones((), jnp.float32))
        light = patches[0, 0] * patches[0, 0] + patches[0, 1] * patches[0, 1]
        return (patch_grad, probe_part, light)

    next_rows = from_behind(object_slices, "row", -1)
    further = from_behind(next_rows, "row", -1)
    window = jnp.concatenate([object_slices, next_rows, further], axis=2)

    def visit_slot(slot_index, running):
        grad_window, probe_grad, illumination = running
        row_start = offsets[slot_index, 0] - first_row
        col_start = offsets[slot_index, 1]
        corner = (anchor, anchor, row_start, col_start)
        patches = lax.dynamic_slice(window, corner, (slices, 2, pixels, pixels))
        patch_grad, probe_part, light = slot_terms(patches, slot_index)
        current = lax.dynamic_slice(grad_window, corner, (slices, 2, pixels, pixels))
        grad_window = lax.dynamic_update_slice(grad_window, current + patch_grad, corner)
        return (grad_window, probe_grad + probe_part, illumination + light)

    start = (
        jnp.zeros(window.shape, jnp.float32),
        jnp.zeros(probe_modes.shape, jnp.float32),
        jnp.zeros((pixels, pixels), jnp.float32),
    )
    grad_window, probe_grad, illumination = lax.fori_loop(0, counts[0], visit_slot, start)
    own_rows = grad_window[:, :, :tile_rows]
    next_part = grad_window[:, :, tile_rows : 2 * tile_rows]
    far_part = grad_window[:, :, 2 * tile_rows :]
    outgoing = next_part + from_behind(far_part, "row", 1)
    from_prev = from_behind(outgoing, "row", 1)
    object_grad = own_rows + from_prev
    flat_grad = probe_grad.reshape(probe_grad.shape[0] * 2, pixels * pixels)
    flat_light = illumination.reshape(1, pixels * pixels)
    summed_grad, summed_light = lax.psum((flat_grad, flat_light), "row")
    flat_step = summed_grad / (summed_light + 1.0)
    probe_step = flat_step.reshape(probe_modes.shape)
    return (object_grad, probe_step)


def solution(mesh):
    in_specs = (
        P(None, None, ("grp", "row"), None),
        P("grp", None, None, None),
        P(),
        P(("grp", "row"), None, None),
        P(("grp", "row"), None),
        P(("grp", "row")),
    )
    out_specs = (P(None, None, ("grp", "row"), None), P("grp", None, None, None))
    return jax.shard_map(local, mesh=mesh, in_specs=in_specs, out_specs=out_specs, check_vma=False)
```

profile of v0, /device:TPU:1, one launch (start us, length us, event | category | flops | bytes accessed | tf_op | source)
XLA Modules:
  0.0 560.0 jit_solution(13188677821572920948)
XLA Ops:
  7.3 26.5 %collective-permute-done = f32[2,2,64,2048]{3,2,1,0:T(8,128)S(1)} collective-permute-done((f32[2,2,64,2048]{3,2,1,0:T(8,128)}, f32[2,2,64,2048]{3,2,1,0:T(8,128)S(1)}, u32[]{:S(2)}, u32[]{:S(2)}) %collective-permute-start) | collective-permute-done | bytes 2097184 | tf_op jit(solution)/shard_map/ppermute | solution.py:11
  33.8 2.8 collective-permute-start.1
  36.6 1.2 copy.188
  37.9 1.1 fusion.372
  39.0 20.4 %collective-permute-done.1 = f32[2,2,64,2048]{3,2,1,0:T(8,128)} collective-permute-done((f32[2,2,64,2048]{3,2,1,0:T(8,128)S(1)}, f32[2,2,64,2048]{3,2,1,0:T(8,128)}, u32[]{:S(2)}, u32[]{:S(2)}) %collective-permute-start.1) | collective-permute-done | bytes 2097184 | tf_op jit(solution)/shard_map/ppermute | solution.py:11
  59.4 5.6 %pad_maximum_fusion = f32[2,2,192,2048]{3,2,1,0:T(8,128)} fusion(f32[2,2,64,2048]{3,2,1,0:T(8,128)} %collective-permute-done.1, f32[2,2,64,2048]{3,2,1,0:T(8,128)S(1)} %collective-permute-done, f32[2,2,64,2048]{3,2,1,0:T(8,128)} %param.8), kind=kLoop, calls=%fused_computation.433 | loop fusion | flops 3145728 | bytes 12582912 | tf_op jit(solution)/shard_map/concatenate | solution.py:90
  65.1 3.4 broadcast_in_dim.15
  68.5 93.0 %while.17 = (s32[]{:T(128)}, f32[2,2,192,2048]{3,2,1,0:T(8,128)}, f32[4,2,128,128]{2,3,0,1:T(8,128)S(1)}, f32[128,128]{1,0:T(8,128)S(1)}, s32[]{:T(128)}, /*inde...) while((s32[]{:T(128)}, f32[2,2,192,2048]{3,2,1,0:T(8,128)}, ...), condition=%wide.region_10.11_spmd.clone.clone, body=%wide.region_0.10_spmd.clone.clone.sunk | while | flops 4853235712 | bytes 47710564 | solution.py:108
  72.3 1.0 dynamic-slice_bitcast_fusion.7
  73.4 1.0 add_add_fusion.6
  77.8 0.7 convolution_subtract_fusion.9
  80.0 0.8 fusion.602
  80.8 0.8 fusion.603
  81.6 0.8 fusion.599
  82.4 0.8 fusion.600
  86.1 0.8 fusion.608
  86.9 0.8 fusion.609
  87.6 0.8 fusion.605
  88.4 0.8 fusion.606
  92.1 0.9 fusion.611
  108.1 0.8 add_bitcast_fusion.9
  109.3 1.1 add_add_fusion.7
  110.5 2.5 dynamic_update_slice.7
  116.9 1.1 dynamic-slice_bitcast_fusion.7
  118.0 1.1 add_add_fusion.6
  124.7 0.8 fusion.602
  125.5 0.8 fusion.603
  126.2 0.8 fusion.599
  127.0 0.8 fusion.600
  130.7 0.8 fusion.608
  131.5 0.8 fusion.609
  132.3 0.8 fusion.605
  133.1 0.8 fusion.606
  136.8 0.9 fusion.611
  152.7 0.8 add_bitcast_fusion.9
  153.9 1.2 add_add_fusion.7
  155.3 3.4 dynamic_update_slice.7
  161.5 3.2 slice.39
  164.7 139.0 %collective-permute-start.2 = (f32[2,2,64,2048]{3,2,1,0:T(8,128)}, f32[2,2,64,2048]{3,2,1,0:T(8,128)}, u32[]{:S(2)}, u32[]{:S(2)}) collective-permute-start(f32[2,2,64,2048]{3,2,1,0:T(8,128)} %slice.39), channel_id=1, source_target_pairs={{0,1},{1,2},{2,3},{3,4},{4,5},{5,6},{6,7},{7,8},{8,9},{9,10},{10,1... | collective-permute-start | bytes 6291464 | tf_op jit(solution)/shard_map/ppermute | solution.py:11
  303.9 1.1 copy.233
  305.0 22.0 %collective-permute-done.2 = f32[2,2,64,2048]{3,2,1,0:T(8,128)} collective-permute-done((f32[2,2,64,2048]{3,2,1,0:T(8,128)}, f32[2,2,64,2048]{3,2,1,0:T(8,128)}, u32[]{:S(2)}, u32[]{:S(2)}) %collective-permute-start.2) | collective-permute-done | bytes 2097184 | tf_op jit(solution)/shard_map/ppermute | solution.py:11
  327.0 3.9 slice_add_fusion
  330.8 123.7 %collective-permute-start.3 = (f32[2,2,64,2048]{3,2,1,0:T(8,128)}, f32[2,2,64,2048]{3,2,1,0:T(8,128)S(1)}, u32[]{:S(2)}, u32[]{:S(2)}) collective-permute-start(f32[2,2,64,2048]{3,2,1,0:T(8,128)} %slice_add_fusion), channel_id=1, source_target_pairs={{0,1},{1,2},{2,3},{3,4},{4,5},{5,6},{6,7},{7,8},{8,9},{9,10},{10,1... | collective-permute-start | bytes 6291464 | tf_op jit(solution)/shard_map/ppermute | solution.py:11
  454.5 92.2 %all-reduce.9.cloned.1.call-done = (f32[8,16384]{1,0:T(8,128)}, f32[1,16384]{1,0:T(1,128)}) async-done(((f32[8,16384]{1,0:T(8,128)}, f32[1,16384]{1,0:T(1,128)}), (f32[8,16384]{1,0:T(8,128)}, f32[1,16384]{1,0:T(1,128)})) %all-reduce.9.cloned.1.call-update) | async-done | bytes 589840 | tf_op jit(solution)/shard_map/psum | solution.py:117
  546.8 0.9 broadcast_add_fusion
  547.7 1.1 divide_bitcast_fusion
  548.8 0.9 copy.231
  549.7 3.2 slice_add_fusion.1
  (108 shorter events, 54.5 us)
Async XLA Ops:
  7.2 539.6 %all-reduce.9.cloned.1.call-start = ((), (), s32[]{:S(2)}) async-start(), calls=%async_computation | async-start | bytes 1179648 | tf_op jit(solution)/shard_map/psum | solution.py:117
  7.2 26.6 %collective-permute-start = (f32[2,2,64,2048]{3,2,1,0:T(8,128)}, f32[2,2,64,2048]{3,2,1,0:T(8,128)S(1)}, u32[]{:S(2)}, u32[]{:S(2)}) collective-permute-start(f32[2,2,64,2048]{3,2,1,0:T(8,128)} %param.8), channel_id=1, source_target_pairs={{0,15},{1,0},{2,1},{3,2},{4,3},{5,4},{6,5},{7,6},{8,7},{9,8},{10,9... | collective-permute-start | bytes 6291464 | tf_op jit(solution)/shard_map/ppermute | solution.py:11
  33.8 25.6 %collective-permute-start.1 = (f32[2,2,64,2048]{3,2,1,0:T(8,128)S(1)}, f32[2,2,64,2048]{3,2,1,0:T(8,128)}, u32[]{:S(2)}, u32[]{:S(2)}) collective-permute-start(f32[2,2,64,2048]{3,2,1,0:T(8,128)S(1)} %collective-permute-done), channel_id=1, source_target_pairs={{0,15},{1,0},{2,1},{3,2},{4,3},{5,4},{6,5},{7,6},{8,7},{9,8},{10,9... | collective-permute-start | bytes 6291464 | tf_op jit(solution)/shard_map/ppermute | solution.py:11
  65.1 3.5 copy-start.1
  161.5 3.2 copy-start
  164.7 162.3 %collective-permute-start.2 = (f32[2,2,64,2048]{3,2,1,0:T(8,128)}, f32[2,2,64,2048]{3,2,1,0:T(8,128)}, u32[]{:S(2)}, u32[]{:S(2)}) collective-permute-start(f32[2,2,64,2048]{3,2,1,0:T(8,128)} %slice.39), channel_id=1, source_target_pairs={{0,1},{1,2},{2,3},{3,4},{4,5},{5,6},{6,7},{7,8},{8,9},{9,10},{10,1... | collective-permute-start | bytes 6291464 | tf_op jit(solution)/shard_map/ppermute | solution.py:11
  330.8 218.8 %collective-permute-start.3 = (f32[2,2,64,2048]{3,2,1,0:T(8,128)}, f32[2,2,64,2048]{3,2,1,0:T(8,128)S(1)}, u32[]{:S(2)}, u32[]{:S(2)}) collective-permute-start(f32[2,2,64,2048]{3,2,1,0:T(8,128)} %slice_add_fusion), channel_id=1, source_target_pairs={{0,1},{1,2},{2,3},{3,4},{4,5},{5,6},{6,7},{7,8},{8,9},{9,10},{10,1... | collective-permute-start | bytes 6291464 | tf_op jit(solution)/shard_map/ppermute | solution.py:11
Sparse Core Ops, SparseCore 0:
  305.1 241.6 all-reduce.8
where the time goes:
time: 562 us; the launch traced here: 560 us
  starting transfers between devices  266 us (47%)
  waiting for transfers between devices  161 us (29%)
  matrix products  66 us (12%)
  local copies, waits for them, and re-layouts  21.6 us (4%)
  other arithmetic  21.2 us (4%)
  between operations  14.4 us (3%)
  loops' own time  10.1 us (2%)
    ppermute x4, starting transfers between devices, from_behind(): lax.ppermute(array, axis, [(i, (i + by) % peers) for i in range(peers)])  266 us
    psum x1, waiting for transfers between devices, local(): summed_grad, summed_light = lax.psum((flat_grad, flat_light), 'row')  92.2 us
    ppermute x4, waiting for transfers between devices, from_behind(): lax.ppermute(array, axis, [(i, (i + by) % peers) for i in range(peers)])  68.9 us
    dot_general x96, matrix products, contract(): return jnp.einsum(form, first, second, precision=lax.Precision.HIGHEST)  66 us
  transfers between devices with their start and end apart: 5, of which 4 were waited for; matrix products, arithmetic and copies ran while one was open for 2% of the time, Pallas kernels for 0%

commit v1 on v0

v1 whole, which is shorter than its diff:
```python
import functools

import jax
import jax.numpy as jnp
import numpy as np
from jax import lax
from jax.experimental import pallas as pl
from jax.experimental.pallas import tpu as pltpu
from jax.sharding import PartitionSpec as P

CHUNKS = (2, 4, 2)
VMEM_LIMIT = 48 * 1024 * 1024
F32 = jnp.float32
BF16 = jnp.bfloat16


def shifted(array, axis, by):
    peers = lax.axis_size(axis)
    return lax.ppermute(array, axis, [(i, (i + by) % peers) for i in range(peers)])


def fourier_blocks(pixels):
    indices = np.arange(pixels)
    angles = 2.0 * np.pi * (indices[:, None] * indices[None, :] % pixels) / pixels
    re = np.cos(angles) / np.sqrt(pixels)
    im = -np.sin(angles) / np.sqrt(pixels)
    left = np.block([[re, -im], [im, re]]).astype(np.float32)
    high = left.astype(BF16)
    low = (left - high.astype(np.float32)).astype(BF16)
    from_left = np.concatenate([high, low, high], axis=1)
    from_right = np.concatenate([high.T, high.T, low.T], axis=0)
    conj_left = np.concatenate([high.T, low.T, high.T], axis=1)
    conj_right = np.concatenate([high, high, low], axis=0)
    return from_left, from_right, conj_left, conj_right


def pieces(array):
    high = array.astype(BF16)
    return high, (array - high.astype(F32)).astype(BF16)


def transform(left, right, waves):
    stacked = jnp.concatenate([jnp.concatenate(wave, axis=0) for wave in waves], axis=1)
    high, low = pieces(stacked)
    half = jnp.dot(left[...], jnp.concatenate([high, high, low], axis=0), preferred_element_type=F32)
    pixels = half.shape[0] // 2
    turned = jnp.concatenate(
        [
            jnp.concatenate([half[:pixels, at : at + pixels], half[pixels:, at : at + pixels]], axis=1)
            for at in (0, pixels)
        ],
        axis=0,
    )
    high, low = pieces(turned)
    whole = jnp.dot(jnp.concatenate([high, low, high], axis=1), right[...], preferred_element_type=F32)
    return [
        (whole[at : at + pixels, :pixels], whole[at : at + pixels, pixels:]) for at in (0, pixels)
    ]


def times(one, two):
    return one[0] * two[0] - one[1] * two[1], one[0] * two[1] + one[1] * two[0]


def conj_times(one, two):
    return one[0] * two[0] + one[1] * two[1], one[0] * two[1] - one[1] * two[0]


def place(column, columns, pixels):
    base = jnp.minimum(column // pixels * pixels, columns - 2 * pixels)
    return pl.multiple_of(base, pixels), column - base


def cut(tile, column, pixels):
    base, shift = place(column, tile.shape[-1], pixels)
    rows = tile.shape[1]
    wide = tile[:, :, pl.ds(base, 2 * pixels)].reshape(-1, 2 * pixels)
    turned = pltpu.roll(wide, 2 * pixels - shift, 1)
    return turned[:, :pixels].reshape(-1, rows, pixels)


def cut_kernel(pixels, meta, tile, *outs):
    slot = 0
    for out in outs:
        for at in range(out.shape[0]):
            out[at] = cut(tile, meta[slot, 1], pixels)
            slot += 1


def add_kernel(pixels, metas, meta_own, meta_mid, meta_far, *refs):
    refs = list(refs)
    out = refs.pop()
    out[...] = jnp.zeros_like(out)
    count = len(refs) // 3
    for meta, group in (
        (meta_mid, refs[:count]),
        (meta_own, refs[count : 2 * count]),
        (meta_far, refs[2 * count :]),
    ):
        first = 0
        for parts in group:
            size = parts.shape[0]

            def add(at, carry, parts=parts, first=first, meta=meta):
                base, shift = place(meta[first + at, 1], out.shape[-1], pixels)
                part = parts[at]
                wide = jnp.concatenate([part, jnp.zeros_like(part)], axis=2)
                turned = pltpu.roll(wide.reshape(-1, 2 * pixels), shift, 1).reshape(wide.shape)
                out[:, :, pl.ds(base, 2 * pixels)] += turned
                return carry

            lax.fori_loop(0, jnp.clip(meta[0, 2] - first, 0, size), add, 0)
            first += size


def slot_kernel(
    first, meta, tile, above, below, target, probe, prop, left, right, conj_left, conj_right, so_far,
    out_above, out_mid, out_below, total, window, patch, grads, exit_wave, far,
):
    size = above.shape[0]
    modes, _, pixels, _ = probe.shape
    rows = above.shape[2]
    total[...] = so_far[...]

    def visit(at, carry):
        row = lax.rem(meta[first + at, 0], rows)
        window[:, :rows] = above[at]
        window[:, rows : 2 * rows] = cut(tile, meta[first + at, 1], pixels)
        window[:, 2 * rows :] = below[at]
        patch[...] = window[:, pl.ds(row, pixels), :]
        total[2 * modes] += patch[0] * patch[0] + patch[1] * patch[1]
        intensity = jnp.zeros((pixels, pixels), F32)
        for pair in range(0, modes, 2):
            both = (pair, pair + 1)
            waves = [times((probe[m, 0], probe[m, 1]), (patch[0], patch[1])) for m in both]
            waves = transform(left, right, waves)
            waves = [times((prop[0], prop[1]), wave) for wave in waves]
            waves = transform(conj_left, conj_right, waves)
            for m, wave in zip(both, waves):
                exit_wave[m, 0], exit_wave[m, 1] = wave
            waves = [times(wave, (patch[2], patch[3])) for wave in waves]
            waves = transform(left, right, waves)
            for m, wave in zip(both, waves):
                far[m, 0], far[m, 1] = wave
                intensity = intensity + wave[0] * wave[0] + wave[1] * wave[1]
        misfit = 2.0 * (intensity - target[at])
        grads[...] = jnp.zeros_like(grads)
        for pair in range(0, modes, 2):
            both = (pair, pair + 1)
            waves = [(misfit * far[m, 0], misfit * far[m, 1]) for m in both]
            waves = transform(conj_left, conj_right, waves)
            for m, wave in zip(both, waves):
                re, im = conj_times((exit_wave[m, 0], exit_wave[m, 1]), wave)
                grads[2] += re
                grads[3] += im
            waves = [conj_times((patch[2], patch[3]), wave) for wave in waves]
            waves = transform(left, right, waves)
            waves = [conj_times((prop[0], prop[1]), wave) for wave in waves]
            waves = transform(conj_left, conj_right, waves)
            for m, wave in zip(both, waves):
                re, im = conj_times((patch[0], patch[1]), wave)
                total[2 * m] += re
                total[2 * m + 1] += im
                re, im = conj_times((probe[m, 0], probe[m, 1]), wave)
                grads[0] += re
                grads[1] += im
        window[...] = jnp.zeros_like(window)
        window[:, pl.ds(row, pixels), :] = grads[...]
        out_above[at] = window[:, :rows]
        out_mid[at] = window[:, rows : 2 * rows]
        out_below[at] = window[:, 2 * rows :]
        return carry

    lax.fori_loop(0, jnp.clip(meta[0, 2] - first, 0, size), visit, 0)


def in_smem():
    return pl.BlockSpec(memory_space=pltpu.SMEM)


def in_vmem():
    return pl.BlockSpec(memory_space=pltpu.VMEM)


def local(object_slices, probe_modes, propagator_phase, measured, offsets, counts):
    slices, _, tile_rows, columns = object_slices.shape
    modes, _, pixels, _ = probe_modes.shape
    slots = measured.shape[0]
    planes = 2 * slices
    peers = lax.axis_size("row")
    params = pltpu.CompilerParams(vmem_limit_bytes=VMEM_LIMIT)
    tile = object_slices.reshape(planes, tile_rows, columns)
    starts = [sum(CHUNKS[:i]) for i in range(len(CHUNKS))]

    meta_own = jnp.concatenate([offsets, jnp.broadcast_to(counts, (slots, 1))], axis=1)
    meta_mid = shifted(meta_own, "row", 1)
    meta_far = shifted(meta_own, "row", 2)

    def strips(meta):
        return pl.pallas_call(
            functools.partial(cut_kernel, pixels),
            out_shape=[jax.ShapeDtypeStruct((size, planes, tile_rows, pixels), F32) for size in CHUNKS],
            in_specs=[in_smem(), in_vmem()],
            out_specs=[in_vmem()] * len(CHUNKS),
            compiler_params=params,
            cost_estimate=pl.CostEstimate(flops=0, bytes_accessed=4 << 20, transcendentals=0),
        )(meta, tile)

    above = [shifted(part, "row", 1) for part in strips(meta_own)]
    below = [shifted(part, "row", -1) for part in strips(meta_far)]
    targets = [
        shifted(measured[at : at + size], "row", 1) for at, size in zip(starts, CHUNKS)
    ]
    prop = jnp.stack([jnp.cos(propagator_phase), jnp.sin(propagator_phase)])
    tables = [jnp.asarray(table) for table in fourier_blocks(pixels)]

    total = jnp.zeros((2 * modes + 1, pixels, pixels), F32)
    mid, back_own, back_far = [], [], []
    for index, (first, size) in enumerate(zip(starts, CHUNKS)):
        strip = jax.ShapeDtypeStruct((size, planes, tile_rows, pixels), F32)
        field = pltpu.VMEM((planes, pixels, pixels), F32)
        to_above, to_mid, to_below, total = pl.pallas_call(
            functools.partial(slot_kernel, first),
            out_shape=[strip, strip, strip, jax.ShapeDtypeStruct(total.shape, F32)],
            in_specs=[in_smem()] + [in_vmem()] * 11,
            out_specs=[in_vmem()] * 4,
            scratch_shapes=[
                pltpu.VMEM((planes, 3 * tile_rows, pixels), F32),
                field,
                field,
                pltpu.VMEM((modes, 2, pixels, pixels), F32),
                pltpu.VMEM((modes, 2, pixels, pixels), F32),
            ],
            compiler_params=params,
            cost_estimate=pl.CostEstimate(
                flops=size * 6 * modes * 3 * 16 * pixels**3, bytes_accessed=8 << 20, transcendentals=0
            ),
        )(meta_mid, tile, above[index], below[index], targets[index], probe_modes, prop, *tables, total)
        mid.append(to_mid)
        back_own.append(shifted(to_above, "row", -1))
        back_far.append(shifted(to_below, "row", 1))

    object_grad = pl.pallas_call(
        functools.partial(add_kernel, pixels, 3),
        out_shape=jax.ShapeDtypeStruct(tile.shape, F32),
        in_specs=[in_smem()] * 3 + [in_vmem()] * (3 * len(CHUNKS)),
        out_specs=in_vmem(),
        compiler_params=params,
        cost_estimate=pl.CostEstimate(flops=0, bytes_accessed=5 << 20, transcendentals=0),
    )(meta_own, meta_mid, meta_far, *mid, *back_own, *back_far).reshape(object_slices.shape)

    share = pixels // peers
    sent = total.reshape(2 * modes + 1, peers, share, pixels).swapaxes(0, 1)
    summed = lax.all_to_all(sent, "row", 0, 0).sum(axis=0)
    step = summed[: 2 * modes] / (summed[2 * modes :] + 1.0)
    spread = lax.all_to_all(jnp.broadcast_to(step, (peers,) + step.shape), "row", 0, 0)
    probe_step = spread.swapaxes(0, 1).reshape(probe_modes.shape)
    return (object_grad, probe_step)


def solution(mesh):
    in_specs = (
        P(None, None, ("grp", "row"), None),
        P("grp", None, None, None),
        P(),
        P(("grp", "row"), None, None),
        P(("grp", "row"), None),
        P(("grp", "row")),
    )
    out_specs = (P(None, None, ("grp", "row"), None), P("grp", None, None, None))
    return jax.shard_map(local, mesh=mesh, in_specs=in_specs, out_specs=out_specs, check_vma=False)
```

time: 562 us -> 160 us (0.28)
  starting transfers between devices: 266 us -> 18.9 us
  waiting for transfers between devices: 161 us -> 41.2 us
  Pallas kernels: 0 us -> 67.9 us
  matrix products: 66 us -> 0 us
  blocking collectives: 0 us -> 21.5 us
  other arithmetic: 21.2 us -> 1.13 us
  local copies, waits for them, and re-layouts: 21.6 us -> 7.37 us
  between operations: 14.4 us -> 1.57 us
  loops' own time: 10.1 us -> 0 us
    ppermute x4 -> x17, starting transfers between devices: 266 us -> 14.6 us  [shifted(): lax.ppermute(array, axis, [(i, (i + by) % peers) for i in range(peers)])]
    psum x1 -> x0, waiting for transfers between devices: 92.2 us -> none  [local(): summed_grad, summed_light = lax.psum((flat_grad, flat_light), 'row')]
    pallas_call x0 -> x6, Pallas kernels: none -> 67.9 us  [the longest x3 61.2 us: local(): pl.pallas_call(functools.partial(slot_kernel, first), out_shape=[strip, s...]
    dot_general x96 -> x0, matrix products: 66 us -> none  [contract(): return jnp.einsum(form, first, second, precision=lax.Precision.HIGHEST)]
    ppermute x4 -> x17, waiting for transfers between devices: 68.9 us -> 41.2 us  [shifted(): lax.ppermute(array, axis, [(i, (i + by) % peers) for i in range(peers)])]
    all_to_all x0 -> x1, blocking collectives: none -> 21.5 us  [local(): summed = lax.all_to_all(sent, 'row', 0, 0).sum(axis=0)]
    add x9 -> x0, other arithmetic: 12.7 us -> none  [the longest x1 3.88 us: local(): outgoing = next_part + from_behind(far_part, 'row', 1)]
    another operation x1 -> x0, loops' own time: 10.1 us -> none  [local(): lax.fori_loop(0, counts[0], visit_slot, start)]
  transfers between devices with their start and end apart: 5 -> 18, of which waited for: 4 -> 4; matrix products, arithmetic and copies ran while one was open for 2% -> 1% of each run, Pallas kernels for 0% -> 33%
where the time goes in v1:
time: 160 us
  Pallas kernels  67.9 us (42%)
  waiting for transfers between devices  41.2 us (26%)
  blocking collectives  21.5 us (13%)
  starting transfers between devices  18.9 us (12%)
  local copies, waits for them, and re-layouts  7.37 us (5%)
    pallas_call x3, Pallas kernels, local(): pl.pallas_call(functools.partial(slot_kernel, first), out_shape=[strip, s...  61.2 us
    ppermute x17, waiting for transfers between devices, shifted(): lax.ppermute(array, axis, [(i, (i + by) % peers) for i in range(peers)])  41.2 us
    all_to_all x1, blocking collectives, local(): summed = lax.all_to_all(sent, 'row', 0, 0).sum(axis=0)  21.5 us
    ppermute x17, starting transfers between devices, shifted(): lax.ppermute(array, axis, [(i, (i + by) % peers) for i in range(peers)])  14.6 us
    all_to_all x1, starting transfers between devices, local(): lax.all_to_all(jnp.broadcast_to(step, (peers,) + step.shape), 'row', 0, 0)  4.36 us
    pallas_call x1, Pallas kernels, local(): pl.pallas_call(functools.partial(add_kernel, pixels, 3), out_shape=jax.Sh...  4.25 us
  transfers between devices with their start and end apart: 18, of which 4 were waited for; matrix products, arithmetic and copies ran while one was open for 1% of the time, Pallas kernels for 33%

profile of v1, /device:TPU:1, one launch (start us, length us, event | category | flops | bytes accessed | tf_op | source)
XLA Modules:
  0.0 159.6 jit_solution(2351337515570879254)
XLA Ops:
  0.6 0.8 copy.15
  2.0 2.1 %collective-permute-start.1 = (s32[8,3]{1,0:T(8,128)S(1)}, s32[8,3]{1,0:T(8,128)S(1)}, u32[]{:S(2)}, u32[]{:S(2)}) collective-permute-start(s32[8,3]{1,0:T(8,128)S(1)} %concatenate.3.meta.meta_own), channel_id=1, source_target_pairs={{0,2},{1,3},{2,4},{3,5},{4,6},{5,7},{6,8},{7,9},{8,10},{9,11},{10,... | collective-permute-start | bytes 296 | tf_op jit(solution)/shard_map/ppermute | solution.py:19
  4.2 2.1 %collective-permute-start = (s32[8,3]{1,0:T(8,128)S(1)}, s32[8,3]{1,0:T(8,128)S(1)}, u32[]{:S(2)}, u32[]{:S(2)}) collective-permute-start(s32[8,3]{1,0:T(8,128)S(1)} %concatenate.3.meta.meta_own), channel_id=1, source_target_pairs={{0,1},{1,2},{2,3},{3,4},{4,5},{5,6},{6,7},{7,8},{8,9},{9,10},{10,1... | collective-permute-start | bytes 296 | tf_op jit(solution)/shard_map/ppermute | solution.py:19
  6.3 1.6 copy-done
  7.8 1.2 shard_map.116
  9.1 0.0 copy-start.2
  9.1 0.0 copy-start.3
  9.1 0.0 copy-start.4
  9.1 0.0 copy-start.5
  9.1 0.0 copy-start.6
  9.1 0.1 collective-permute-start.2
  9.2 1.1 fusion.1
  10.3 1.5 collective-permute-start.4
  11.9 0.1 collective-permute-start.5
  12.0 1.2 shard_map.117
  13.2 0.4 collective-permute-start.3
  13.7 0.2 cosine_bitcast_fusion
  13.9 0.0 collective-permute-done.meta.meta_mid
  13.9 3.0 %collective-permute-start.6 = (f32[4,4,64,128]{3,2,1,0:T(8,128)S(1)}, f32[4,4,64,128]{3,2,1,0:T(8,128)S(1)}, u32[]{:S(2)}, u32[]{:S(2)}) collective-permute-start(f32[4,4,64,128]{3,2,1,0:T(8,128)S(1)} %get-tuple-element.24), channel_id=1, source_target_pairs={{0,15},{1,0},{2,1},{3,2},{4,3},{5,4},{6,5},{7,6},{8,7},{9,8},{10,9... | collective-permute-start | bytes 1572872 | tf_op jit(solution)/shard_map/ppermute | solution.py:19
  17.0 0.1 collective-permute-start.7
  17.0 0.0 collective-permute-done.2.above
  17.0 0.1 collective-permute-start.8
  17.1 15.6 %collective-permute-done.3.below = f32[2,4,64,128]{3,2,1,0:T(8,128)S(1)} collective-permute-done((f32[2,4,64,128]{3,2,1,0:T(8,128)S(1)}, f32[2,4,64,128]{3,2,1,0:T(8,128)S(1)}, u32[]{:S(2)}, u32[]{:S(2)}) %collective-permute-start.3) | collective-permute-done | bytes 262176 | tf_op jit(solution)/shard_map/ppermute | solution.py:19
  32.7 0.0 collective-permute-start.10
  32.8 15.6 %shard_map.118 = (f32[2,4,64,128]{3,2,1,0:T(8,128)S(1)}, f32[2,4,64,128]{3,2,1,0:T(8,128)S(1)}, f32[2,4,64,128]{3,2,1,0:T(8,128)S(1)}, f32[9,128,128]{2,1,0:T(8,128)S(1)}) custom-call(s32[8,3]{1,0:T(8,128)S(1)} %collective-permute-done.meta.meta_mid, f32[4,64,2048]{2,1,0:T(8,128)} %bitcast.18, f32[2,4,64,128]{3,2,1,0:T(8,128)S(1)} %collective-permute-done.2.above, ...), custom_call_target="tpu_custom_call" | custom-call | flops 4831838208 | bytes 8388608 | tf_op jit(solution)/shard_map/pallas_call | solution.py:222
  48.5 0.0 copy-start.7
  48.5 0.8 copy-done.7
  49.3 0.0 collective-permute-done.7.target
  49.3 0.0 collective-permute-start.9
  49.3 0.0 collective-permute-done.5.above
  49.3 0.0 collective-permute-done.6.below
  49.3 29.7 %shard_map.119 = (f32[4,4,64,128]{3,2,1,0:T(8,128)S(1)}, f32[4,4,64,128]{3,2,1,0:T(8,128)S(1)}, f32[4,4,64,128]{3,2,1,0:T(8,128)S(1)}, f32[9,128,128]{2,1,0:T(8,128)S(1)}) custom-call(s32[8,3]{1,0:T(8,128)S(1)} %collective-permute-done.meta.meta_mid, f32[4,64,2048]{2,1,0:T(8,128)} %bitcast.19, f32[4,4,64,128]{3,2,1,0:T(8,128)S(1)} %collective-permute-done.5.above, ...), custom_call_target="tpu_custom_call" | custom-call | flops 9663676416 | bytes 8388608 | tf_op jit(solution)/shard_map/pallas_call | solution.py:222
  79.1 0.0 collective-permute-done.10.target
  79.1 15.8 %shard_map.120 = (f32[2,4,64,128]{3,2,1,0:T(8,128)S(1)}, f32[2,4,64,128]{3,2,1,0:T(8,128)S(1)}, f32[2,4,64,128]{3,2,1,0:T(8,128)S(1)}, f32[9,128,128]{2,1,0:T(8,128)S(1)}) custom-call(s32[8,3]{1,0:T(8,128)S(1)} %collective-permute-done.meta.meta_mid, f32[4,64,2048]{2,1,0:T(8,128)} %bitcast.20, f32[2,4,64,128]{3,2,1,0:T(8,128)S(1)} %collective-permute-done.8.above, ...), custom_call_target="tpu_custom_call" | custom-call | flops 4831838208 | bytes 8388608 | tf_op jit(solution)/shard_map/pallas_call | solution.py:222
  95.0 21.5 %all_to_all.10 = f32[16,9,8,128]{3,2,1,0:T(8,128)} all-to-all(f32[16,9,8,128]{3,2,1,0:T(8,128)S(1)} %copy_bitcast_fusion), channel_id=1, replica_groups=mesh['grp'=2,'row'=16] {'row'}, dimensions={0} | all-to-all | bytes 1179648 | tf_op jit(solution)/shard_map/all_to_all | solution.py:254
  116.5 1.1 reduce_sum.9
  117.6 0.8 broadcast_in_dim.8
  118.5 4.4 %all-to-all-start.1 = ((f32[16,8,8,128]{3,2,1,0:T(8,128)}), f32[16,8,8,128]{3,2,1,0:T(8,128)}, u32[]{:S(2)}, u32[]{:S(2)}) async-start(f32[16,8,8,128]{3,2,1,0:T(8,128)} %broadcast_in_dim.8), calls=%async_computation.1 | async-start | bytes 1048576 | tf_op jit(solution)/shard_map/all_to_all | solution.py:256
  122.8 0.3 collective-permute-start.11
  123.2 4.2 %collective-permute-start.12 = (f32[4,4,64,128]{3,2,1,0:T(8,128)S(1)}, f32[4,4,64,128]{3,2,1,0:T(8,128)S(1)}, u32[]{:S(2)}, u32[]{:S(2)}) collective-permute-start(f32[4,4,64,128]{3,2,1,0:T(8,128)S(1)} %get-tuple-element.32), channel_id=1, source_target_pairs={{0,15},{1,0},{2,1},{3,2},{4,3},{5,4},{6,5},{7,6},{8,7},{9,8},{10,9... | collective-permute-start | bytes 1572872 | tf_op jit(solution)/shard_map/ppermute | solution.py:19
  127.4 0.0 collective-permute-start.15
  127.4 0.5 collective-permute-start.13
  127.9 4.5 %collective-permute-done.11.refs_3_ = f32[2,4,64,128]{3,2,1,0:T(8,128)S(1)} collective-permute-done((f32[2,4,64,128]{3,2,1,0:T(8,128)S(1)}, f32[2,4,64,128]{3,2,1,0:T(8,128)S(1)}, u32[]{:S(2)}, u32[]{:S(2)}) %collective-permute-start.11) | collective-permute-done | bytes 262176 | tf_op jit(solution)/shard_map/ppermute | solution.py:19
  132.5 18.2 %collective-permute-done.14.refs_6_ = f32[2,4,64,128]{3,2,1,0:T(8,128)S(1)} collective-permute-done((f32[2,4,64,128]{3,2,1,0:T(8,128)S(1)}, f32[2,4,64,128]{3,2,1,0:T(8,128)S(1)}, u32[]{:S(2)}, u32[]{:S(2)}) %collective-permute-start.14) | collective-permute-done | bytes 262176 | tf_op jit(solution)/shard_map/ppermute | solution.py:19
  150.7 2.8 %collective-permute-done.13.refs_5_ = f32[2,4,64,128]{3,2,1,0:T(8,128)S(1)} collective-permute-done((f32[2,4,64,128]{3,2,1,0:T(8,128)S(1)}, f32[2,4,64,128]{3,2,1,0:T(8,128)S(1)}, u32[]{:S(2)}, u32[]{:S(2)}) %collective-permute-start.13) | collective-permute-done | bytes 262176 | tf_op jit(solution)/shard_map/ppermute | solution.py:19
  153.5 0.0 collective-permute-done.16.refs_8_
  153.5 4.2 %shard_map.121 = f32[4,64,2048]{2,1,0:T(8,128)} custom-call(s32[8,3]{1,0:T(8,128)S(1)} %concatenate.3.meta.meta_own, s32[8,3]{1,0:T(8,128)S(1)} %collective-permute-done.meta.meta_mid, s32[8,3]{1,0:T(8,128)S(1)} %collective-permute-done.1.meta.meta_far, f32[2,4,64,128]{3,2,1,0:T(8,128)S(1)} %get-tuple-element.22.refs_0_, ...), custom_call_target="tpu_custom_call" | custom-call | bytes 5242880 | tf_op jit(solution)/shard_map/pallas_call | solution.py:243
  157.8 1.9 %copy.17 = f32[16,8,8,128]{3,2,0,1:T(8,128)} copy(f32[16,8,8,128]{3,2,1,0:T(8,128)} %all-to-all-done.1) | data formatting | bytes 1048576 | tf_op jit(solution)/shard_map/all_to_all | solution.py:256
  (28 shorter events, 0.2 us)
Async XLA Ops:
  2.0 10.0 %collective-permute-start.1 = (s32[8,3]{1,0:T(8,128)S(1)}, s32[8,3]{1,0:T(8,128)S(1)}, u32[]{:S(2)}, u32[]{:S(2)}) collective-permute-start(s32[8,3]{1,0:T(8,128)S(1)} %concatenate.3.meta.meta_own), channel_id=1, source_target_pairs={{0,2},{1,3},{2,4},{3,5},{4,6},{5,7},{6,8},{7,9},{8,10},{9,11},{10,... | collective-permute-start | bytes 296 | tf_op jit(solution)/shard_map/ppermute | solution.py:19
  4.2 9.8 %collective-permute-start = (s32[8,3]{1,0:T(8,128)S(1)}, s32[8,3]{1,0:T(8,128)S(1)}, u32[]{:S(2)}, u32[]{:S(2)}) collective-permute-start(s32[8,3]{1,0:T(8,128)S(1)} %concatenate.3.meta.meta_own), channel_id=1, source_target_pairs={{0,1},{1,2},{2,3},{3,4},{4,5},{5,6},{6,7},{7,8},{8,9},{9,10},{10,1... | collective-permute-start | bytes 296 | tf_op jit(solution)/shard_map/ppermute | solution.py:19
  6.2 1.6 copy-start
  7.8 4.2 %copy-start.1 = (f32[2,2,64,2048]{3,2,1,0:T(8,128)S(1)}, f32[2,2,64,2048]{3,2,1,0:T(8,128)}, u32[]{:S(2)}) copy-start(f32[2,2,64,2048]{3,2,1,0:T(8,128)} %param.10) | copy-start | bytes 6291460
  7.8 5.8 %copy-start.9 = (f32[128,128]{1,0:T(8,128)S(1)}, f32[128,128]{1,0:T(8,128)}, u32[]{:S(2)}) copy-start(f32[128,128]{1,0:T(8,128)} %param.12) | copy-start | bytes 196612
  7.8 6.1 %copy-start.8 = (f32[8,128,128]{2,1,0:T(8,128)S(1)}, f32[8,128,128]{2,1,0:T(8,128)}, u32[]{:S(2)}) copy-start(f32[8,128,128]{2,1,0:T(8,128)} %param.13) | copy-start | bytes 1572868
  9.1 23.7 %copy-start.2 = (f32[4,2,128,128]{3,2,1,0:T(8,128)S(1)}, f32[4,2,128,128]{3,2,1,0:T(8,128)}, u32[]{:S(2)}) copy-start(f32[4,2,128,128]{3,2,1,0:T(8,128)} %probe.5) | copy-start | bytes 1572868
  9.1 23.7 %copy-start.3 = (bf16[768,256]{1,0:T(8,128)(2,1)S(1)}, bf16[768,256]{1,0:T(8,128)(2,1)}, u32[]{:S(2)}) copy-start(bf16[768,256]{1,0:T(8,128)(2,1)} %constant.14.clone.right) | copy-start | bytes 1179652
  9.1 23.7 %copy-start.4 = (bf16[256,768]{1,0:T(8,128)(2,1)S(1)}, bf16[256,768]{1,0:T(8,128)(2,1)}, u32[]{:S(2)}) copy-start(bf16[256,768]{1,0:T(8,128)(2,1)} %constant.15.clone.conj_left) | copy-start | bytes 1179652
  9.1 23.7 %copy-start.5 = (bf16[768,256]{1,0:T(8,128)(2,1)S(1)}, bf16[768,256]{1,0:T(8,128)(2,1)}, u32[]{:S(2)}) copy-start(bf16[768,256]{1,0:T(8,128)(2,1)} %constant.16.clone.conj_right) | copy-start | bytes 1179652
  9.1 23.7 %copy-start.6 = (bf16[256,768]{1,0:T(8,128)(2,1)S(1)}, bf16[256,768]{1,0:T(8,128)(2,1)}, u32[]{:S(2)}) copy-start(bf16[256,768]{1,0:T(8,128)(2,1)} %constant.5.clone.left) | copy-start | bytes 1179652
  9.1 7.9 %collective-permute-start.2 = (f32[2,4,64,128]{3,2,1,0:T(8,128)S(1)}, f32[2,4,64,128]{3,2,1,0:T(8,128)S(1)}, u32[]{:S(2)}, u32[]{:S(2)}) collective-permute-start(f32[2,4,64,128]{3,2,1,0:T(8,128)S(1)} %get-tuple-element.20), channel_id=1, source_target_pairs={{0,1},{1,2},{2,3},{3,4},{4,5},{5,6},{6,7},{7,8},{8,9},{9,10},{10,1... | collective-permute-start | bytes 786440 | tf_op jit(solution)/shard_map/ppermute | solution.py:19
  10.3 6.6 %collective-permute-start.4 = (f32[2,128,128]{2,1,0:T(8,128)S(1)}, f32[2,128,128]{2,1,0:T(8,128)S(1)}, u32[]{:S(2)}, u32[]{:S(2)}) collective-permute-start(f32[2,128,128]{2,1,0:T(8,128)S(1)} %get-tuple-element.39), channel_id=1, source_target_pairs={{0,1},{1,2},{2,3},{3,4},{4,5},{5,6},{6,7},{7,8},{8,9},{9,10},{10,1... | collective-permute-start | bytes 393224 | tf_op jit(solution)/shard_map/ppermute | solution.py:19
  11.9 37.4 %collective-permute-start.5 = (f32[4,4,64,128]{3,2,1,0:T(8,128)S(1)}, f32[4,4,64,128]{3,2,1,0:T(8,128)S(1)}, u32[]{:S(2)}, u32[]{:S(2)}) collective-permute-start(f32[4,4,64,128]{3,2,1,0:T(8,128)S(1)} %get-tuple-element.23), channel_id=1, source_target_pairs={{0,1},{1,2},{2,3},{3,4},{4,5},{5,6},{6,7},{7,8},{8,9},{9,10},{10,1... | collective-permute-start | bytes 1572872 | tf_op jit(solution)/shard_map/ppermute | solution.py:19
  13.2 19.5 %collective-permute-start.3 = (f32[2,4,64,128]{3,2,1,0:T(8,128)S(1)}, f32[2,4,64,128]{3,2,1,0:T(8,128)S(1)}, u32[]{:S(2)}, u32[]{:S(2)}) collective-permute-start(f32[2,4,64,128]{3,2,1,0:T(8,128)S(1)} %get-tuple-element.21), channel_id=1, source_target_pairs={{0,15},{1,0},{2,1},{3,2},{4,3},{5,4},{6,5},{7,6},{8,7},{9,8},{10,9... | collective-permute-start | bytes 786440 | tf_op jit(solution)/shard_map/ppermute | solution.py:19
  13.9 35.4 %collective-permute-start.6 = (f32[4,4,64,128]{3,2,1,0:T(8,128)S(1)}, f32[4,4,64,128]{3,2,1,0:T(8,128)S(1)}, u32[]{:S(2)}, u32[]{:S(2)}) collective-permute-start(f32[4,4,64,128]{3,2,1,0:T(8,128)S(1)} %get-tuple-element.24), channel_id=1, source_target_pairs={{0,15},{1,0},{2,1},{3,2},{4,3},{5,4},{6,5},{7,6},{8,7},{9,8},{10,9... | collective-permute-start | bytes 1572872 | tf_op jit(solution)/shard_map/ppermute | solution.py:19
  17.0 32.3 %collective-permute-start.7 = (f32[4,128,128]{2,1,0:T(8,128)S(1)}, f32[4,128,128]{2,1,0:T(8,128)S(1)}, u32[]{:S(2)}, u32[]{:S(2)}) collective-permute-start(f32[4,128,128]{2,1,0:T(8,128)S(1)} %slice.16), channel_id=1, source_target_pairs={{0,1},{1,2},{2,3},{3,4},{4,5},{5,6},{6,7},{7,8},{8,9},{9,10},{10,1... | collective-permute-start | bytes 786440 | tf_op jit(solution)/shard_map/ppermute | solution.py:19
  17.0 62.0 %collective-permute-start.8 = (f32[2,4,64,128]{3,2,1,0:T(8,128)S(1)}, f32[2,4,64,128]{3,2,1,0:T(8,128)S(1)}, u32[]{:S(2)}, u32[]{:S(2)}) collective-permute-start(f32[2,4,64,128]{3,2,1,0:T(8,128)S(1)} %get-tuple-element.27), channel_id=1, source_target_pairs={{0,1},{1,2},{2,3},{3,4},{4,5},{5,6},{6,7},{7,8},{8,9},{9,10},{10,1... | collective-permute-start | bytes 786440 | tf_op jit(solution)/shard_map/ppermute | solution.py:19
  32.7 46.3 %collective-permute-start.10 = (f32[2,128,128]{2,1,0:T(8,128)S(1)}, f32[2,128,128]{2,1,0:T(8,128)S(1)}, u32[]{:S(2)}, u32[]{:S(2)}) collective-permute-start(f32[2,128,128]{2,1,0:T(8,128)S(1)} %get-tuple-element.38), channel_id=1, source_target_pairs={{0,1},{1,2},{2,3},{3,4},{4,5},{5,6},{6,7},{7,8},{8,9},{9,10},{10,1... | collective-permute-start | bytes 393224 | tf_op jit(solution)/shard_map/ppermute | solution.py:19
  48.5 0.8 copy-start.7
  49.3 29.8 %collective-permute-start.9 = (f32[2,4,64,128]{3,2,1,0:T(8,128)S(1)}, f32[2,4,64,128]{3,2,1,0:T(8,128)S(1)}, u32[]{:S(2)}, u32[]{:S(2)}) collective-permute-start(f32[2,4,64,128]{3,2,1,0:T(8,128)S(1)} %get-tuple-element.28), channel_id=1, source_target_pairs={{0,15},{1,0},{2,1},{3,2},{4,3},{5,4},{6,5},{7,6},{8,7},{9,8},{10,9... | collective-permute-start | bytes 786440 | tf_op jit(solution)/shard_map/ppermute | solution.py:19
  118.5 39.3 %all-to-all-start.1 = ((f32[16,8,8,128]{3,2,1,0:T(8,128)}), f32[16,8,8,128]{3,2,1,0:T(8,128)}, u32[]{:S(2)}, u32[]{:S(2)}) async-start(f32[16,8,8,128]{3,2,1,0:T(8,128)} %broadcast_in_dim.8), calls=%async_computation.1 | async-start | bytes 1048576 | tf_op jit(solution)/shard_map/all_to_all | solution.py:256
  122.8 9.6 %collective-permute-start.11 = (f32[2,4,64,128]{3,2,1,0:T(8,128)S(1)}, f32[2,4,64,128]{3,2,1,0:T(8,128)S(1)}, u32[]{:S(2)}, u32[]{:S(2)}) collective-permute-start(f32[2,4,64,128]{3,2,1,0:T(8,128)S(1)} %get-tuple-element.31), channel_id=1, source_target_pairs={{0,15},{1,0},{2,1},{3,2},{4,3},{5,4},{6,5},{7,6},{8,7},{9,8},{10,9... | collective-permute-start | bytes 786440 | tf_op jit(solution)/shard_map/ppermute | solution.py:19
  123.2 30.3 %collective-permute-start.12 = (f32[4,4,64,128]{3,2,1,0:T(8,128)S(1)}, f32[4,4,64,128]{3,2,1,0:T(8,128)S(1)}, u32[]{:S(2)}, u32[]{:S(2)}) collective-permute-start(f32[4,4,64,128]{3,2,1,0:T(8,128)S(1)} %get-tuple-element.32), channel_id=1, source_target_pairs={{0,15},{1,0},{2,1},{3,2},{4,3},{5,4},{6,5},{7,6},{8,7},{9,8},{10,9... | collective-permute-start | bytes 1572872 | tf_op jit(solution)/shard_map/ppermute | solution.py:19
  127.4 26.1 %collective-permute-start.15 = (f32[4,4,64,128]{3,2,1,0:T(8,128)S(1)}, f32[4,4,64,128]{3,2,1,0:T(8,128)S(1)}, u32[]{:S(2)}, u32[]{:S(2)}) collective-permute-start(f32[4,4,64,128]{3,2,1,0:T(8,128)S(1)} %get-tuple-element.35), channel_id=1, source_target_pairs={{0,1},{1,2},{2,3},{3,4},{4,5},{5,6},{6,7},{7,8},{8,9},{9,10},{10,1... | collective-permute-start | bytes 1572872 | tf_op jit(solution)/shard_map/ppermute | solution.py:19
  127.4 23.3 %collective-permute-start.14 = (f32[2,4,64,128]{3,2,1,0:T(8,128)S(1)}, f32[2,4,64,128]{3,2,1,0:T(8,128)S(1)}, u32[]{:S(2)}, u32[]{:S(2)}) collective-permute-start(f32[2,4,64,128]{3,2,1,0:T(8,128)S(1)} %get-tuple-element.34), channel_id=1, source_target_pairs={{0,1},{1,2},{2,3},{3,4},{4,5},{5,6},{6,7},{7,8},{8,9},{9,10},{10,1... | collective-permute-start | bytes 786440 | tf_op jit(solution)/shard_map/ppermute | solution.py:19
  127.4 26.1 %collective-permute-start.13 = (f32[2,4,64,128]{3,2,1,0:T(8,128)S(1)}, f32[2,4,64,128]{3,2,1,0:T(8,128)S(1)}, u32[]{:S(2)}, u32[]{:S(2)}) collective-permute-start(f32[2,4,64,128]{3,2,1,0:T(8,128)S(1)} %get-tuple-element.33), channel_id=1, source_target_pairs={{0,15},{1,0},{2,1},{3,2},{4,3},{5,4},{6,5},{7,6},{8,7},{9,8},{10,9... | collective-permute-start | bytes 786440 | tf_op jit(solution)/shard_map/ppermute | solution.py:19
  132.5 21.0 %collective-permute-start.16 = (f32[2,4,64,128]{3,2,1,0:T(8,128)S(1)}, f32[2,4,64,128]{3,2,1,0:T(8,128)S(1)}, u32[]{:S(2)}, u32[]{:S(2)}) collective-permute-start(f32[2,4,64,128]{3,2,1,0:T(8,128)S(1)} %get-tuple-element.36), channel_id=1, source_target_pairs={{0,1},{1,2},{2,3},{3,4},{4,5},{5,6},{6,7},{7,8},{8,9},{9,10},{10,1... | collective-permute-start | bytes 786440 | tf_op jit(solution)/shard_map/ppermute | solution.py:19

commit v2 on v1

--- a/solution.py
+++ b/solution.py
@@ -9,6 +9,7 @@
 from jax.sharding import PartitionSpec as P
 
 CHUNKS = (2, 4, 2)
+BATCH = 2
 VMEM_LIMIT = 48 * 1024 * 1024
 F32 = jnp.float32
 BF16 = jnp.bfloat16
@@ -44,18 +45,17 @@
     high, low = pieces(stacked)
     half = jnp.dot(left[...], jnp.concatenate([high, high, low], axis=0), preferred_element_type=F32)
     pixels = half.shape[0] // 2
+    places = [i * pixels for i in range(len(waves))]
     turned = jnp.concatenate(
         [
             jnp.concatenate([half[:pixels, at : at + pixels], half[pixels:, at : at + pixels]], axis=1)
-            for at in (0, pixels)
+            for at in places
         ],
         axis=0,
     )
     high, low = pieces(turned)
     whole = jnp.dot(jnp.concatenate([high, low, high], axis=1), right[...], preferred_element_type=F32)
-    return [
-        (whole[at : at + pixels, :pixels], whole[at : at + pixels, pixels:]) for at in (0, pixels)
-    ]
+    return [(whole[at : at + pixels, :pixels], whole[at : at + pixels, pixels:]) for at in places]
 
 
 def times(one, two):
@@ -121,57 +121,59 @@
     modes, _, pixels, _ = probe.shape
     rows = above.shape[2]
     total[...] = so_far[...]
-
-    def visit(at, carry):
-        row = lax.rem(meta[first + at, 0], rows)
-        window[:, :rows] = above[at]
-        window[:, rows : 2 * rows] = cut(tile, meta[first + at, 1], pixels)
-        window[:, 2 * rows :] = below[at]
-        patch[...] = window[:, pl.ds(row, pixels), :]
-        total[2 * modes] += patch[0] * patch[0] + patch[1] * patch[1]
-        intensity = jnp.zeros((pixels, pixels), F32)
-        for pair in range(0, modes, 2):
-            both = (pair, pair + 1)
-            waves = [times((probe[m, 0], probe[m, 1]), (patch[0], patch[1])) for m in both]
-            waves = transform(left, right, waves)
-            waves = [times((prop[0], prop[1]), wave) for wave in waves]
-            waves = transform(conj_left, conj_right, waves)
-            for m, wave in zip(both, waves):
-                exit_wave[m, 0], exit_wave[m, 1] = wave
-            waves = [times(wave, (patch[2], patch[3])) for wave in waves]
-            waves = transform(left, right, waves)
-            for m, wave in zip(both, waves):
-                far[m, 0], far[m, 1] = wave
-                intensity = intensity + wave[0] * wave[0] + wave[1] * wave[1]
-        misfit = 2.0 * (intensity - target[at])
+    held = [(s, m) for s in range(BATCH) for m in range(modes)]
+    live_slots = jnp.clip(meta[0, 2] - first, 0, size)
+
+    def visit(step, carry):
+        slots = [step * BATCH + s for s in range(BATCH)]
+        starts = [lax.rem(meta[first + at, 0], rows) for at in slots]
+        live = [jnp.where(at < live_slots, 1.0, 0.0).astype(F32) for at in slots]
+        for s, at in enumerate(slots):
+            window[:, :rows] = above[at]
+            window[:, rows : 2 * rows] = cut(tile, meta[first + at, 1], pixels)
+            window[:, 2 * rows :] = below[at]
+            patch[s] = window[:, pl.ds(starts[s], pixels), :]
+            total[2 * modes] += live[s] * (patch[s, 0] * patch[s, 0] + patch[s, 1] * patch[s, 1])
+        waves = [times((probe[m, 0], probe[m, 1]), (patch[s, 0], patch[s, 1])) for s, m in held]
+        waves = transform(left, right, waves)
+        waves = [times((prop[0], prop[1]), wave) for wave in waves]
+        waves = transform(conj_left, conj_right, waves)
+        for (s, m), wave in zip(held, waves):
+            exit_wave[s, m, 0], exit_wave[s, m, 1] = wave
+        waves = [times(wave, (patch[s, 2], patch[s, 3])) for (s, m), wave in zip(held, waves)]
+        waves = transform(left, right, waves)
+        intensity = [jnp.zeros((pixels, pixels), F32)] * BATCH
+        for (s, m), wave in zip(held, waves):
+            far[s, m, 0], far[s, m, 1] = wave
+            intensity[s] = intensity[s] + wave[0] * wave[0] + wave[1] * wave[1]
+        misfit = [2.0 * live[s] * (intensity[s] - target[at]) for s, at in enumerate(slots)]
+        waves = [(misfit[s] * far[s, m, 0], misfit[s] * far[s, m, 1]) for s, m in held]
+        waves = transform(conj_left, conj_right, waves)
         grads[...] = jnp.zeros_like(grads)
-        for pair in range(0, modes, 2):
-            both = (pair, pair + 1)
-            waves = [(misfit * far[m, 0], misfit * far[m, 1]) for m in both]
-            waves = transform(conj_left, conj_right, waves)
-            for m, wave in zip(both, waves):
-                re, im = conj_times((exit_wave[m, 0], exit_wave[m, 1]), wave)
-                grads[2] += re
-                grads[3] += im
-            waves = [conj_times((patch[2], patch[3]), wave) for wave in waves]
-            waves = transform(left, right, waves)
-            waves = [conj_times((prop[0], prop[1]), wave) for wave in waves]
-            waves = transform(conj_left, conj_right, waves)
-            for m, wave in zip(both, waves):
-                re, im = conj_times((patch[0], patch[1]), wave)
-                total[2 * m] += re
-                total[2 * m + 1] += im
-                re, im = conj_times((probe[m, 0], probe[m, 1]), wave)
-                grads[0] += re
-                grads[1] += im
-        window[...] = jnp.zeros_like(window)
-        window[:, pl.ds(row, pixels), :] = grads[...]
-        out_above[at] = window[:, :rows]
-        out_mid[at] = window[:, rows : 2 * rows]
-        out_below[at] = window[:, 2 * rows :]
+        for (s, m), wave in zip(held, waves):
+            re, im = conj_times((exit_wave[s, m, 0], exit_wave[s, m, 1]), wave)
+            grads[s, 2] += re
+            grads[s, 3] += im
+        waves = [conj_times((patch[s, 2], patch[s, 3]), wave) for (s, m), wave in zip(held, waves)]
+        waves = transform(left, right, waves)
+        waves = [conj_times((prop[0], prop[1]), wave) for wave in waves]
+        waves = transform(conj_left, conj_right, waves)
+        for (s, m), wave in zip(held, waves):
+            re, im = conj_times((patch[s, 0], patch[s, 1]), wave)
+            total[2 * m] += re
+            total[2 * m + 1] += im
+            re, im = conj_times((probe[m, 0], probe[m, 1]), wave)
+            grads[s, 0] += re
+            grads[s, 1] += im
+        for s, at in enumerate(slots):
+            window[...] = jnp.zeros_like(window)
+            window[:, pl.ds(starts[s], pixels), :] = grads[s]
+            out_above[at] = window[:, :rows]
+            out_mid[at] = window[:, rows : 2 * rows]
+            out_below[at] = window[:, 2 * rows :]
         return carry
 
-    lax.fori_loop(0, jnp.clip(meta[0, 2] - first, 0, size), visit, 0)
+    lax.fori_loop(0, (live_slots + BATCH - 1) // BATCH, visit, 0)
 
 
 def in_smem():
@@ -218,7 +220,8 @@
     mid, back_own, back_far = [], [], []
     for index, (first, size) in enumerate(zip(starts, CHUNKS)):
         strip = jax.ShapeDtypeStruct((size, planes, tile_rows, pixels), F32)
-        field = pltpu.VMEM((planes, pixels, pixels), F32)
+        field = pltpu.VMEM((BATCH, planes, pixels, pixels), F32)
+        kept = pltpu.VMEM((BATCH, modes, 2, pixels, pixels), F32)
         to_above, to_mid, to_below, total = pl.pallas_call(
             functools.partial(slot_kernel, first),
             out_shape=[strip, strip, strip, jax.ShapeDtypeStruct(total.shape, F32)],
@@ -228,8 +231,8 @@
                 pltpu.VMEM((planes, 3 * tile_rows, pixels), F32),
                 field,
                 field,
-                pltpu.VMEM((modes, 2, pixels, pixels), F32),
-                pltpu.VMEM((modes, 2, pixels, pixels), F32),
+                kept,
+                kept,
             ],
             compiler_params=params,
             cost_estimate=pl.CostEstimate(

time: 160 us -> 141 us (0.88)
  Pallas kernels: 67.9 us -> 31.3 us
  blocking collectives: 21.5 us -> 38.2 us
    pallas_call x3, Pallas kernels: 61.2 us -> 23.5 us  [local(): pl.pallas_call(functools.partial(slot_kernel, first), out_shape=[strip, s...]
    all_to_all x1, blocking collectives: 21.5 us -> 38.2 us  [local(): summed = lax.all_to_all(sent, 'row', 0, 0).sum(axis=0)]
  transfers between devices with their start and end apart: 18 -> 18, of which waited for: 4 -> 4; matrix products, arithmetic and copies ran while one was open for 1% -> 1% of each run, Pallas kernels for 33% -> 21%
where the time goes in v2:
time: 141 us; the launch traced here: 140 us
  waiting for transfers between devices  41.2 us (29%)
  blocking collectives  38.2 us (27%)
  Pallas kernels  31.3 us (22%)
  starting transfers between devices  19.4 us (14%)
  local copies, waits for them, and re-layouts  7.37 us (5%)
  between operations  1.56 us (1%)
    ppermute x17, waiting for transfers between devices, shifted(): lax.ppermute(array, axis, [(i, (i + by) % peers) for i in range(peers)])  41.2 us
    all_to_all x1, blocking collectives, local(): summed = lax.all_to_all(sent, 'row', 0, 0).sum(axis=0)  38.2 us
    pallas_call x3, Pallas kernels, local(): pl.pallas_call(functools.partial(slot_kernel, first), out_shape=[strip, s...  23.5 us
    ppermute x17, starting transfers between devices, shifted(): lax.ppermute(array, axis, [(i, (i + by) % peers) for i in range(peers)])  15.1 us
    pallas_call x1, Pallas kernels, local(): pl.pallas_call(functools.partial(add_kernel, pixels, 3), out_shape=jax.Sh...  5.33 us
    all_to_all x1, starting transfers between devices, local(): lax.all_to_all(jnp.broadcast_to(step, (peers,) + step.shape), 'row', 0, 0)  4.36 us
    unnamed x21, local copies, waits for them, and re-layouts  3.2 us
  transfers between devices with their start and end apart: 18, of which 4 were waited for; matrix products, arithmetic and copies ran while one was open for 1% of the time, Pallas kernels for 21%

profile of v2, /device:TPU:1, one launch (start us, length us, event | category | flops | bytes accessed | tf_op | source)
XLA Modules:
  0.0 140.2 jit_solution(1680967666797344475)
XLA Ops:
  0.6 0.8 copy.15
  2.0 2.1 %collective-permute-start.1 = (s32[8,3]{1,0:T(8,128)S(1)}, s32[8,3]{1,0:T(8,128)S(1)}, u32[]{:S(2)}, u32[]{:S(2)}) collective-permute-start(s32[8,3]{1,0:T(8,128)S(1)} %concatenate.3.meta.meta_own), channel_id=1, source_target_pairs={{0,2},{1,3},{2,4},{3,5},{4,6},{5,7},{6,8},{7,9},{8,10},{9,11},{10,... | collective-permute-start | bytes 296 | tf_op jit(solution)/shard_map/ppermute | solution.py:20
  4.2 2.1 %collective-permute-start = (s32[8,3]{1,0:T(8,128)S(1)}, s32[8,3]{1,0:T(8,128)S(1)}, u32[]{:S(2)}, u32[]{:S(2)}) collective-permute-start(s32[8,3]{1,0:T(8,128)S(1)} %concatenate.3.meta.meta_own), channel_id=1, source_target_pairs={{0,1},{1,2},{2,3},{3,4},{4,5},{5,6},{6,7},{7,8},{8,9},{9,10},{10,1... | collective-permute-start | bytes 296 | tf_op jit(solution)/shard_map/ppermute | solution.py:20
  6.3 1.6 %copy-done = f32[2,2,64,2048]{3,2,1,0:T(8,128)S(1)} copy-done((f32[2,2,64,2048]{3,2,1,0:T(8,128)S(1)}, f32[2,2,64,2048]{3,2,1,0:T(8,128)}, u32[]{:S(2)}) %copy-start) | copy-done | bytes 2097176
  7.8 1.2 shard_map.116
  9.1 0.0 copy-start.2
  9.1 0.0 copy-start.3
  9.1 0.0 copy-start.4
  9.1 0.0 copy-start.5
  9.1 0.0 copy-start.6
  9.1 0.1 collective-permute-start.2
  9.2 1.1 fusion.1
  10.3 1.5 %collective-permute-start.4 = (f32[2,128,128]{2,1,0:T(8,128)S(1)}, f32[2,128,128]{2,1,0:T(8,128)S(1)}, u32[]{:S(2)}, u32[]{:S(2)}) collective-permute-start(f32[2,128,128]{2,1,0:T(8,128)S(1)} %get-tuple-element.39), channel_id=1, source_target_pairs={{0,1},{1,2},{2,3},{3,4},{4,5},{5,6},{6,7},{7,8},{8,9},{9,10},{10,1... | collective-permute-start | bytes 393224 | tf_op jit(solution)/shard_map/ppermute | solution.py:20
  11.9 0.1 collective-permute-start.5
  12.0 0.0 collective-permute-done.1.meta.meta_far
  12.0 1.2 shard_map.117
  13.2 0.4 collective-permute-start.3
  13.7 0.2 cosine_bitcast_fusion
  14.0 3.0 %collective-permute-start.6 = (f32[4,4,64,128]{3,2,1,0:T(8,128)S(1)}, f32[4,4,64,128]{3,2,1,0:T(8,128)S(1)}, u32[]{:S(2)}, u32[]{:S(2)}) collective-permute-start(f32[4,4,64,128]{3,2,1,0:T(8,128)S(1)} %get-tuple-element.24), channel_id=1, source_target_pairs={{0,15},{1,0},{2,1},{3,2},{4,3},{5,4},{6,5},{7,6},{8,7},{9,8},{10,9... | collective-permute-start | bytes 1572872 | tf_op jit(solution)/shard_map/ppermute | solution.py:20
  17.0 0.0 collective-permute-done.4.target
  17.0 0.1 collective-permute-start.7
  17.0 0.1 collective-permute-start.8
  17.1 15.6 %collective-permute-done.3.below = f32[2,4,64,128]{3,2,1,0:T(8,128)S(1)} collective-permute-done((f32[2,4,64,128]{3,2,1,0:T(8,128)S(1)}, f32[2,4,64,128]{3,2,1,0:T(8,128)S(1)}, u32[]{:S(2)}, u32[]{:S(2)}) %collective-permute-start.3) | collective-permute-done | bytes 262176 | tf_op jit(solution)/shard_map/ppermute | solution.py:20
  32.7 0.0 collective-permute-start.10
  32.8 10.7 %shard_map.118 = (f32[2,4,64,128]{3,2,1,0:T(8,128)S(1)}, f32[2,4,64,128]{3,2,1,0:T(8,128)S(1)}, f32[2,4,64,128]{3,2,1,0:T(8,128)S(1)}, f32[9,128,128]{2,1,0:T(8,128)S(1)}) custom-call(s32[8,3]{1,0:T(8,128)S(1)} %collective-permute-done.meta.meta_mid, f32[4,64,2048]{2,1,0:T(8,128)} %bitcast.18, f32[2,4,64,128]{3,2,1,0:T(8,128)S(1)} %collective-permute-done.2.above, ...), custom_call_target="tpu_custom_call" | custom-call | flops 4831838208 | bytes 8388608 | tf_op jit(solution)/shard_map/pallas_call | solution.py:225
  43.5 0.0 copy-start.7
  43.5 0.8 copy-done.7
  44.3 0.0 collective-permute-done.7.target
  44.3 0.5 collective-permute-start.9
  44.9 11.0 %shard_map.119 = (f32[4,4,64,128]{3,2,1,0:T(8,128)S(1)}, f32[4,4,64,128]{3,2,1,0:T(8,128)S(1)}, f32[4,4,64,128]{3,2,1,0:T(8,128)S(1)}, f32[9,128,128]{2,1,0:T(8,128)S(1)}) custom-call(s32[8,3]{1,0:T(8,128)S(1)} %collective-permute-done.meta.meta_mid, f32[4,64,2048]{2,1,0:T(8,128)} %bitcast.19, f32[4,4,64,128]{3,2,1,0:T(8,128)S(1)} %collective-permute-done.5.above, ...), custom_call_target="tpu_custom_call" | custom-call | flops 9663676416 | bytes 8388608 | tf_op jit(solution)/shard_map/pallas_call | solution.py:225
  55.8 0.0 collective-permute-done.10.target
  55.8 0.0 collective-permute-done.8.above
  55.9 1.9 %shard_map.120 = (f32[2,4,64,128]{3,2,1,0:T(8,128)S(1)}, f32[2,4,64,128]{3,2,1,0:T(8,128)S(1)}, f32[2,4,64,128]{3,2,1,0:T(8,128)S(1)}, f32[9,128,128]{2,1,0:T(8,128)S(1)}) custom-call(s32[8,3]{1,0:T(8,128)S(1)} %collective-permute-done.meta.meta_mid, f32[4,64,2048]{2,1,0:T(8,128)} %bitcast.20, f32[2,4,64,128]{3,2,1,0:T(8,128)S(1)} %collective-permute-done.8.above, ...), custom_call_target="tpu_custom_call" | custom-call | flops 4831838208 | bytes 8388608 | tf_op jit(solution)/shard_map/pallas_call | solution.py:225
  57.8 38.2 %all_to_all.10 = f32[16,9,8,128]{3,2,1,0:T(8,128)} all-to-all(f32[16,9,8,128]{3,2,1,0:T(8,128)S(1)} %copy_bitcast_fusion), channel_id=1, replica_groups=mesh['grp'=2,'row'=16] {'row'}, dimensions={0} | all-to-all | bytes 1179648 | tf_op jit(solution)/shard_map/all_to_all | solution.py:257
  96.0 1.1 reduce_sum.9
  97.1 0.8 broadcast_in_dim.8
  98.0 4.4 %all-to-all-start.1 = ((f32[16,8,8,128]{3,2,1,0:T(8,128)}), f32[16,8,8,128]{3,2,1,0:T(8,128)}, u32[]{:S(2)}, u32[]{:S(2)}) async-start(f32[16,8,8,128]{3,2,1,0:T(8,128)} %broadcast_in_dim.8), calls=%async_computation.1 | async-start | bytes 1048576 | tf_op jit(solution)/shard_map/all_to_all | solution.py:259
  102.3 0.3 collective-permute-start.11
  102.7 4.2 %collective-permute-start.12 = (f32[4,4,64,128]{3,2,1,0:T(8,128)S(1)}, f32[4,4,64,128]{3,2,1,0:T(8,128)S(1)}, u32[]{:S(2)}, u32[]{:S(2)}) collective-permute-start(f32[4,4,64,128]{3,2,1,0:T(8,128)S(1)} %get-tuple-element.32), channel_id=1, source_target_pairs={{0,15},{1,0},{2,1},{3,2},{4,3},{5,4},{6,5},{7,6},{8,7},{9,8},{10,9... | collective-permute-start | bytes 1572872 | tf_op jit(solution)/shard_map/ppermute | solution.py:20
  106.9 0.0 collective-permute-start.15
  106.9 0.0 collective-permute-start.14
  106.9 0.5 collective-permute-start.13
  107.4 4.5 %collective-permute-done.11.refs_3_ = f32[2,4,64,128]{3,2,1,0:T(8,128)S(1)} collective-permute-done((f32[2,4,64,128]{3,2,1,0:T(8,128)S(1)}, f32[2,4,64,128]{3,2,1,0:T(8,128)S(1)}, u32[]{:S(2)}, u32[]{:S(2)}) %collective-permute-start.11) | collective-permute-done | bytes 262176 | tf_op jit(solution)/shard_map/ppermute | solution.py:20
  111.9 18.2 %collective-permute-done.14.refs_6_ = f32[2,4,64,128]{3,2,1,0:T(8,128)S(1)} collective-permute-done((f32[2,4,64,128]{3,2,1,0:T(8,128)S(1)}, f32[2,4,64,128]{3,2,1,0:T(8,128)S(1)}, u32[]{:S(2)}, u32[]{:S(2)}) %collective-permute-start.14) | collective-permute-done | bytes 262176 | tf_op jit(solution)/shard_map/ppermute | solution.py:20
  130.2 2.8 %collective-permute-done.13.refs_5_ = f32[2,4,64,128]{3,2,1,0:T(8,128)S(1)} collective-permute-done((f32[2,4,64,128]{3,2,1,0:T(8,128)S(1)}, f32[2,4,64,128]{3,2,1,0:T(8,128)S(1)}, u32[]{:S(2)}, u32[]{:S(2)}) %collective-permute-start.13) | collective-permute-done | bytes 262176 | tf_op jit(solution)/shard_map/ppermute | solution.py:20
  133.0 0.0 collective-permute-done.16.refs_8_
  133.0 5.3 %shard_map.121 = f32[4,64,2048]{2,1,0:T(8,128)} custom-call(s32[8,3]{1,0:T(8,128)S(1)} %concatenate.3.meta.meta_own, s32[8,3]{1,0:T(8,128)S(1)} %collective-permute-done.meta.meta_mid, s32[8,3]{1,0:T(8,128)S(1)} %collective-permute-done.1.meta.meta_far, f32[2,4,64,128]{3,2,1,0:T(8,128)S(1)} %get-tuple-element.22.refs_0_, ...), custom_call_target="tpu_custom_call" | custom-call | bytes 5242880 | tf_op jit(solution)/shard_map/pallas_call | solution.py:246
  138.3 1.9 %copy.17 = f32[16,8,8,128]{3,2,0,1:T(8,128)} copy(f32[16,8,8,128]{3,2,1,0:T(8,128)} %all-to-all-done.1) | data formatting | bytes 1048576 | tf_op jit(solution)/shard_map/all_to_all | solution.py:259
  (28 shorter events, 0.2 us)
Async XLA Ops:
  2.0 10.0 %collective-permute-start.1 = (s32[8,3]{1,0:T(8,128)S(1)}, s32[8,3]{1,0:T(8,128)S(1)}, u32[]{:S(2)}, u32[]{:S(2)}) collective-permute-start(s32[8,3]{1,0:T(8,128)S(1)} %concatenate.3.meta.meta_own), channel_id=1, source_target_pairs={{0,2},{1,3},{2,4},{3,5},{4,6},{5,7},{6,8},{7,9},{8,10},{9,11},{10,... | collective-permute-start | bytes 296 | tf_op jit(solution)/shard_map/ppermute | solution.py:20
  4.2 9.8 %collective-permute-start = (s32[8,3]{1,0:T(8,128)S(1)}, s32[8,3]{1,0:T(8,128)S(1)}, u32[]{:S(2)}, u32[]{:S(2)}) collective-permute-start(s32[8,3]{1,0:T(8,128)S(1)} %concatenate.3.meta.meta_own), channel_id=1, source_target_pairs={{0,1},{1,2},{2,3},{3,4},{4,5},{5,6},{6,7},{7,8},{8,9},{9,10},{10,1... | collective-permute-start | bytes 296 | tf_op jit(solution)/shard_map/ppermute | solution.py:20
  6.2 1.6 %copy-start = (f32[2,2,64,2048]{3,2,1,0:T(8,128)S(1)}, f32[2,2,64,2048]{3,2,1,0:T(8,128)}, u32[]{:S(2)}) copy-start(f32[2,2,64,2048]{3,2,1,0:T(8,128)} %param.10) | copy-start | bytes 6291460
  7.8 4.2 %copy-start.1 = (f32[2,2,64,2048]{3,2,1,0:T(8,128)S(1)}, f32[2,2,64,2048]{3,2,1,0:T(8,128)}, u32[]{:S(2)}) copy-start(f32[2,2,64,2048]{3,2,1,0:T(8,128)} %param.10) | copy-start | bytes 6291460
  7.8 5.8 %copy-start.9 = (f32[128,128]{1,0:T(8,128)S(1)}, f32[128,128]{1,0:T(8,128)}, u32[]{:S(2)}) copy-start(f32[128,128]{1,0:T(8,128)} %param.12) | copy-start | bytes 196612
  7.8 6.1 %copy-start.8 = (f32[8,128,128]{2,1,0:T(8,128)S(1)}, f32[8,128,128]{2,1,0:T(8,128)}, u32[]{:S(2)}) copy-start(f32[8,128,128]{2,1,0:T(8,128)} %param.13) | copy-start | bytes 1572868
  9.1 23.7 %copy-start.2 = (f32[4,2,128,128]{3,2,1,0:T(8,128)S(1)}, f32[4,2,128,128]{3,2,1,0:T(8,128)}, u32[]{:S(2)}) copy-start(f32[4,2,128,128]{3,2,1,0:T(8,128)} %probe.5) | copy-start | bytes 1572868
  9.1 23.7 %copy-start.3 = (bf16[768,256]{1,0:T(8,128)(2,1)S(1)}, bf16[768,256]{1,0:T(8,128)(2,1)}, u32[]{:S(2)}) copy-start(bf16[768,256]{1,0:T(8,128)(2,1)} %constant.14.clone.right) | copy-start | bytes 1179652
  9.1 23.7 %copy-start.4 = (bf16[256,768]{1,0:T(8,128)(2,1)S(1)}, bf16[256,768]{1,0:T(8,128)(2,1)}, u32[]{:S(2)}) copy-start(bf16[256,768]{1,0:T(8,128)(2,1)} %constant.15.clone.conj_left) | copy-start | bytes 1179652
  9.1 23.7 %copy-start.5 = (bf16[768,256]{1,0:T(8,128)(2,1)S(1)}, bf16[768,256]{1,0:T(8,128)(2,1)}, u32[]{:S(2)}) copy-start(bf16[768,256]{1,0:T(8,128)(2,1)} %constant.16.clone.conj_right) | copy-start | bytes 1179652
  9.1 23.7 %copy-start.6 = (bf16[256,768]{1,0:T(8,128)(2,1)S(1)}, bf16[256,768]{1,0:T(8,128)(2,1)}, u32[]{:S(2)}) copy-start(bf16[256,768]{1,0:T(8,128)(2,1)} %constant.5.clone.left) | copy-start | bytes 1179652
  9.1 7.9 %collective-permute-start.2 = (f32[2,4,64,128]{3,2,1,0:T(8,128)S(1)}, f32[2,4,64,128]{3,2,1,0:T(8,128)S(1)}, u32[]{:S(2)}, u32[]{:S(2)}) collective-permute-start(f32[2,4,64,128]{3,2,1,0:T(8,128)S(1)} %get-tuple-element.20), channel_id=1, source_target_pairs={{0,1},{1,2},{2,3},{3,4},{4,5},{5,6},{6,7},{7,8},{8,9},{9,10},{10,1... | collective-permute-start | bytes 786440 | tf_op jit(solution)/shard_map/ppermute | solution.py:20
  10.3 6.6 %collective-permute-start.4 = (f32[2,128,128]{2,1,0:T(8,128)S(1)}, f32[2,128,128]{2,1,0:T(8,128)S(1)}, u32[]{:S(2)}, u32[]{:S(2)}) collective-permute-start(f32[2,128,128]{2,1,0:T(8,128)S(1)} %get-tuple-element.39), channel_id=1, source_target_pairs={{0,1},{1,2},{2,3},{3,4},{4,5},{5,6},{6,7},{7,8},{8,9},{9,10},{10,1... | collective-permute-start | bytes 393224 | tf_op jit(solution)/shard_map/ppermute | solution.py:20
  11.9 33.0 %collective-permute-start.5 = (f32[4,4,64,128]{3,2,1,0:T(8,128)S(1)}, f32[4,4,64,128]{3,2,1,0:T(8,128)S(1)}, u32[]{:S(2)}, u32[]{:S(2)}) collective-permute-start(f32[4,4,64,128]{3,2,1,0:T(8,128)S(1)} %get-tuple-element.23), channel_id=1, source_target_pairs={{0,1},{1,2},{2,3},{3,4},{4,5},{5,6},{6,7},{7,8},{8,9},{9,10},{10,1... | collective-permute-start | bytes 1572872 | tf_op jit(solution)/shard_map/ppermute | solution.py:20
  13.2 19.5 %collective-permute-start.3 = (f32[2,4,64,128]{3,2,1,0:T(8,128)S(1)}, f32[2,4,64,128]{3,2,1,0:T(8,128)S(1)}, u32[]{:S(2)}, u32[]{:S(2)}) collective-permute-start(f32[2,4,64,128]{3,2,1,0:T(8,128)S(1)} %get-tuple-element.21), channel_id=1, source_target_pairs={{0,15},{1,0},{2,1},{3,2},{4,3},{5,4},{6,5},{7,6},{8,7},{9,8},{10,9... | collective-permute-start | bytes 786440 | tf_op jit(solution)/shard_map/ppermute | solution.py:20
  14.0 30.9 %collective-permute-start.6 = (f32[4,4,64,128]{3,2,1,0:T(8,128)S(1)}, f32[4,4,64,128]{3,2,1,0:T(8,128)S(1)}, u32[]{:S(2)}, u32[]{:S(2)}) collective-permute-start(f32[4,4,64,128]{3,2,1,0:T(8,128)S(1)} %get-tuple-element.24), channel_id=1, source_target_pairs={{0,15},{1,0},{2,1},{3,2},{4,3},{5,4},{6,5},{7,6},{8,7},{9,8},{10,9... | collective-permute-start | bytes 1572872 | tf_op jit(solution)/shard_map/ppermute | solution.py:20
  17.0 27.4 %collective-permute-start.7 = (f32[4,128,128]{2,1,0:T(8,128)S(1)}, f32[4,128,128]{2,1,0:T(8,128)S(1)}, u32[]{:S(2)}, u32[]{:S(2)}) collective-permute-start(f32[4,128,128]{2,1,0:T(8,128)S(1)} %slice.16), channel_id=1, source_target_pairs={{0,1},{1,2},{2,3},{3,4},{4,5},{5,6},{6,7},{7,8},{8,9},{9,10},{10,1... | collective-permute-start | bytes 786440 | tf_op jit(solution)/shard_map/ppermute | solution.py:20
  17.0 38.8 %collective-permute-start.8 = (f32[2,4,64,128]{3,2,1,0:T(8,128)S(1)}, f32[2,4,64,128]{3,2,1,0:T(8,128)S(1)}, u32[]{:S(2)}, u32[]{:S(2)}) collective-permute-start(f32[2,4,64,128]{3,2,1,0:T(8,128)S(1)} %get-tuple-element.27), channel_id=1, source_target_pairs={{0,1},{1,2},{2,3},{3,4},{4,5},{5,6},{6,7},{7,8},{8,9},{9,10},{10,1... | collective-permute-start | bytes 786440 | tf_op jit(solution)/shard_map/ppermute | solution.py:20
  32.7 23.1 %collective-permute-start.10 = (f32[2,128,128]{2,1,0:T(8,128)S(1)}, f32[2,128,128]{2,1,0:T(8,128)S(1)}, u32[]{:S(2)}, u32[]{:S(2)}) collective-permute-start(f32[2,128,128]{2,1,0:T(8,128)S(1)} %get-tuple-element.38), channel_id=1, source_target_pairs={{0,1},{1,2},{2,3},{3,4},{4,5},{5,6},{6,7},{7,8},{8,9},{9,10},{10,1... | collective-permute-start | bytes 393224 | tf_op jit(solution)/shard_map/ppermute | solution.py:20
  43.5 0.8 copy-start.7
  44.3 11.5 %collective-permute-start.9 = (f32[2,4,64,128]{3,2,1,0:T(8,128)S(1)}, f32[2,4,64,128]{3,2,1,0:T(8,128)S(1)}, u32[]{:S(2)}, u32[]{:S(2)}) collective-permute-start(f32[2,4,64,128]{3,2,1,0:T(8,128)S(1)} %get-tuple-element.28), channel_id=1, source_target_pairs={{0,15},{1,0},{2,1},{3,2},{4,3},{5,4},{6,5},{7,6},{8,7},{9,8},{10,9... | collective-permute-start | bytes 786440 | tf_op jit(solution)/shard_map/ppermute | solution.py:20
  98.0 40.4 %all-to-all-start.1 = ((f32[16,8,8,128]{3,2,1,0:T(8,128)}), f32[16,8,8,128]{3,2,1,0:T(8,128)}, u32[]{:S(2)}, u32[]{:S(2)}) async-start(f32[16,8,8,128]{3,2,1,0:T(8,128)} %broadcast_in_dim.8), calls=%async_computation.1 | async-start | bytes 1048576 | tf_op jit(solution)/shard_map/all_to_all | solution.py:259
  102.3 9.6 %collective-permute-start.11 = (f32[2,4,64,128]{3,2,1,0:T(8,128)S(1)}, f32[2,4,64,128]{3,2,1,0:T(8,128)S(1)}, u32[]{:S(2)}, u32[]{:S(2)}) collective-permute-start(f32[2,4,64,128]{3,2,1,0:T(8,128)S(1)} %get-tuple-element.31), channel_id=1, source_target_pairs={{0,15},{1,0},{2,1},{3,2},{4,3},{5,4},{6,5},{7,6},{8,7},{9,8},{10,9... | collective-permute-start | bytes 786440 | tf_op jit(solution)/shard_map/ppermute | solution.py:20
  102.7 30.3 %collective-permute-start.12 = (f32[4,4,64,128]{3,2,1,0:T(8,128)S(1)}, f32[4,4,64,128]{3,2,1,0:T(8,128)S(1)}, u32[]{:S(2)}, u32[]{:S(2)}) collective-permute-start(f32[4,4,64,128]{3,2,1,0:T(8,128)S(1)} %get-tuple-element.32), channel_id=1, source_target_pairs={{0,15},{1,0},{2,1},{3,2},{4,3},{5,4},{6,5},{7,6},{8,7},{9,8},{10,9... | collective-permute-start | bytes 1572872 | tf_op jit(solution)/shard_map/ppermute | solution.py:20
  106.9 26.1 %collective-permute-start.15 = (f32[4,4,64,128]{3,2,1,0:T(8,128)S(1)}, f32[4,4,64,128]{3,2,1,0:T(8,128)S(1)}, u32[]{:S(2)}, u32[]{:S(2)}) collective-permute-start(f32[4,4,64,128]{3,2,1,0:T(8,128)S(1)} %get-tuple-element.35), channel_id=1, source_target_pairs={{0,1},{1,2},{2,3},{3,4},{4,5},{5,6},{6,7},{7,8},{8,9},{9,10},{10,1... | collective-permute-start | bytes 1572872 | tf_op jit(solution)/shard_map/ppermute | solution.py:20
  106.9 23.3 %collective-permute-start.14 = (f32[2,4,64,128]{3,2,1,0:T(8,128)S(1)}, f32[2,4,64,128]{3,2,1,0:T(8,128)S(1)}, u32[]{:S(2)}, u32[]{:S(2)}) collective-permute-start(f32[2,4,64,128]{3,2,1,0:T(8,128)S(1)} %get-tuple-element.34), channel_id=1, source_target_pairs={{0,1},{1,2},{2,3},{3,4},{4,5},{5,6},{6,7},{7,8},{8,9},{9,10},{10,1... | collective-permute-start | bytes 786440 | tf_op jit(solution)/shard_map/ppermute | solution.py:20
  106.9 26.1 %collective-permute-start.13 = (f32[2,4,64,128]{3,2,1,0:T(8,128)S(1)}, f32[2,4,64,128]{3,2,1,0:T(8,128)S(1)}, u32[]{:S(2)}, u32[]{:S(2)}) collective-permute-start(f32[2,4,64,128]{3,2,1,0:T(8,128)S(1)} %get-tuple-element.33), channel_id=1, source_target_pairs={{0,15},{1,0},{2,1},{3,2},{4,3},{5,4},{6,5},{7,6},{8,7},{9,8},{10,9... | collective-permute-start | bytes 786440 | tf_op jit(solution)/shard_map/ppermute | solution.py:20
  111.9 21.0 %collective-permute-start.16 = (f32[2,4,64,128]{3,2,1,0:T(8,128)S(1)}, f32[2,4,64,128]{3,2,1,0:T(8,128)S(1)}, u32[]{:S(2)}, u32[]{:S(2)}) collective-permute-start(f32[2,4,64,128]{3,2,1,0:T(8,128)S(1)} %get-tuple-element.36), channel_id=1, source_target_pairs={{0,1},{1,2},{2,3},{3,4},{4,5},{5,6},{6,7},{7,8},{8,9},{9,10},{10,1... | collective-permute-start | bytes 786440 | tf_op jit(solution)/shard_map/ppermute | solution.py:20

commit v3 on v2

--- a/solution.py
+++ b/solution.py
@@ -20,7 +20,7 @@
     return lax.ppermute(array, axis, [(i, (i + by) % peers) for i in range(peers)])
 
 
-def fourier_blocks(pixels):
+def fourier_tables(pixels):
     indices = np.arange(pixels)
     angles = 2.0 * np.pi * (indices[:, None] * indices[None, :] % pixels) / pixels
     re = np.cos(angles) / np.sqrt(pixels)
@@ -28,11 +28,7 @@
     left = np.block([[re, -im], [im, re]]).astype(np.float32)
     high = left.astype(BF16)
     low = (left - high.astype(np.float32)).astype(BF16)
-    from_left = np.concatenate([high, low, high], axis=1)
-    from_right = np.concatenate([high.T, high.T, low.T], axis=0)
-    conj_left = np.concatenate([high.T, low.T, high.T], axis=1)
-    conj_right = np.concatenate([high, high, low], axis=0)
-    return from_left, from_right, conj_left, conj_right
+    return np.stack([high, low, high.T, low.T])
 
 
 def pieces(array):
@@ -40,10 +36,13 @@
     return high, (array - high.astype(F32)).astype(BF16)
 
 
-def transform(left, right, waves):
+def transform(tables, conj, waves):
+    at_left, at_right = (2, 0) if conj else (0, 2)
+    left = jnp.concatenate([tables[at_left], tables[at_left + 1], tables[at_left]], axis=1)
+    right = jnp.concatenate([tables[at_right], tables[at_right], tables[at_right + 1]], axis=0)
     stacked = jnp.concatenate([jnp.concatenate(wave, axis=0) for wave in waves], axis=1)
     high, low = pieces(stacked)
-    half = jnp.dot(left[...], jnp.concatenate([high, high, low], axis=0), preferred_element_type=F32)
+    half = jnp.dot(left, jnp.concatenate([high, high, low], axis=0), preferred_element_type=F32)
     pixels = half.shape[0] // 2
     places = [i * pixels for i in range(len(waves))]
     turned = jnp.concatenate(
@@ -54,7 +53,7 @@
         axis=0,
     )
     high, low = pieces(turned)
-    whole = jnp.dot(jnp.concatenate([high, low, high], axis=1), right[...], preferred_element_type=F32)
+    whole = jnp.dot(jnp.concatenate([high, low, high], axis=1), right, preferred_element_type=F32)
     return [(whole[at : at + pixels, :pixels], whole[at : at + pixels, pixels:]) for at in places]
 
 
@@ -79,15 +78,22 @@
     return turned[:, :pixels].reshape(-1, rows, pixels)
 
 
-def cut_kernel(pixels, meta, tile, *outs):
+def cut_kernel(pixels, extra, meta, tile, *refs):
+    if extra:
+        measured, *outs = refs
+    else:
+        outs = refs
+    planes, rows, _ = tile.shape
     slot = 0
     for out in outs:
         for at in range(out.shape[0]):
-            out[at] = cut(tile, meta[slot, 1], pixels)
+            out[at, :planes] = cut(tile, meta[slot, 1], pixels)
+            if extra:
+                out[at, planes:] = measured[slot].reshape(-1, rows, pixels)
             slot += 1
 
 
-def add_kernel(pixels, metas, meta_own, meta_mid, meta_far, *refs):
+def add_kernel(pixels, meta_own, meta_mid, meta_far, *refs):
     refs = list(refs)
     out = refs.pop()
     out[...] = jnp.zeros_like(out)
@@ -114,10 +120,12 @@
 
 
 def slot_kernel(
-    first, meta, tile, above, below, target, probe, prop, left, right, conj_left, conj_right, so_far,
-    out_above, out_mid, out_below, total, window, patch, grads, exit_wave, far,
+    first, meta, tile, above, below, probe, prop, tables, so_far,
+    out_above, out_mid, out_below, total, *refs,
 ):
+    shares, (window, patch, grads, exit_wave, far) = refs[:-5], refs[-5:]
     size = above.shape[0]
+    planes = tile.shape[0]
     modes, _, pixels, _ = probe.shape
     rows = above.shape[2]
     total[...] = so_far[...]
@@ -129,35 +137,35 @@
         starts = [lax.rem(meta[first + at, 0], rows) for at in slots]
         live = [jnp.where(at < live_slots, 1.0, 0.0).astype(F32) for at in slots]
         for s, at in enumerate(slots):
-            window[:, :rows] = above[at]
+            window[:, :rows] = above[at, :planes]
             window[:, rows : 2 * rows] = cut(tile, meta[first + at, 1], pixels)
             window[:, 2 * rows :] = below[at]
             patch[s] = window[:, pl.ds(starts[s], pixels), :]
             total[2 * modes] += live[s] * (patch[s, 0] * patch[s, 0] + patch[s, 1] * patch[s, 1])
         waves = [times((probe[m, 0], probe[m, 1]), (patch[s, 0], patch[s, 1])) for s, m in held]
-        waves = transform(left, right, waves)
+        waves = transform(tables, False, waves)
         waves = [times((prop[0], prop[1]), wave) for wave in waves]
-        waves = transform(conj_left, conj_right, waves)
+        waves = transform(tables, True, waves)
         for (s, m), wave in zip(held, waves):
             exit_wave[s, m, 0], exit_wave[s, m, 1] = wave
         waves = [times(wave, (patch[s, 2], patch[s, 3])) for (s, m), wave in zip(held, waves)]
-        waves = transform(left, right, waves)
+        waves = transform(tables, False, waves)
         intensity = [jnp.zeros((pixels, pixels), F32)] * BATCH
         for (s, m), wave in zip(held, waves):
             far[s, m, 0], far[s, m, 1] = wave
             intensity[s] = intensity[s] + wave[0] * wave[0] + wave[1] * wave[1]
-        misfit = [2.0 * live[s] * (intensity[s] - target[at]) for s, at in enumerate(slots)]
+        misfit = [2.0 * live[s] * (intensity[s] - above[at, planes:].reshape(pixels, pixels)) for s, at in enumerate(slots)]
         waves = [(misfit[s] * far[s, m, 0], misfit[s] * far[s, m, 1]) for s, m in held]
-        waves = transform(conj_left, conj_right, waves)
+        waves = transform(tables, True, waves)
         grads[...] = jnp.zeros_like(grads)
         for (s, m), wave in zip(held, waves):
             re, im = conj_times((exit_wave[s, m, 0], exit_wave[s, m, 1]), wave)
             grads[s, 2] += re
             grads[s, 3] += im
         waves = [conj_times((patch[s, 2], patch[s, 3]), wave) for (s, m), wave in zip(held, waves)]
-        waves = transform(left, right, waves)
+        waves = transform(tables, False, waves)
         waves = [conj_times((prop[0], prop[1]), wave) for wave in waves]
-        waves = transform(conj_left, conj_right, waves)
+        waves = transform(tables, True, waves)
         for (s, m), wave in zip(held, waves):
             re, im = conj_times((patch[s, 0], patch[s, 1]), wave)
             total[2 * m] += re
@@ -175,6 +183,30 @@
 
     lax.fori_loop(0, (live_slots + BATCH - 1) // BATCH, visit, 0)
 
+    if shares:
+        own, other = shares
+        chips, _, share, _ = own.shape
+        core = lax.rem(meta[0, 0] // rows + 1, 2)
+        for chip in range(chips):
+            for plane in range(2 * modes + 1):
+                own[chip, plane] = total[plane, pl.ds((2 * chip + core) * share, share)]
+                other[chip, plane] = total[plane, pl.ds((2 * chip + 1 - core) * share, share)]
+
+
+def step_kernel(parts, out):
+    summed = parts[0]
+    for at in range(1, parts.shape[0]):
+        summed = summed + parts[at]
+    step = summed[:-1] / (summed[-1:] + 1.0)
+    for at in range(out.shape[0]):
+        out[at] = step
+
+
+def order_kernel(parts, out):
+    share = parts.shape[2]
+    for at in range(parts.shape[0]):
+        out[:, at * share : (at + 1) * share] = parts[at]
+
 
 def in_smem():
     return pl.BlockSpec(memory_space=pltpu.SMEM)
@@ -195,56 +227,76 @@
     starts = [sum(CHUNKS[:i]) for i in range(len(CHUNKS))]
 
     meta_own = jnp.concatenate([offsets, jnp.broadcast_to(counts, (slots, 1))], axis=1)
-    meta_mid = shifted(meta_own, "row", 1)
     meta_far = shifted(meta_own, "row", 2)
 
-    def strips(meta):
+    def strips(meta, *extra):
+        rest = sum(part.size // (slots * tile_rows * pixels) for part in extra)
         return pl.pallas_call(
-            functools.partial(cut_kernel, pixels),
-            out_shape=[jax.ShapeDtypeStruct((size, planes, tile_rows, pixels), F32) for size in CHUNKS],
-            in_specs=[in_smem(), in_vmem()],
+            functools.partial(cut_kernel, pixels, bool(extra)),
+            out_shape=[
+                jax.ShapeDtypeStruct((size, planes + rest, tile_rows, pixels), F32) for size in CHUNKS
+            ],
+            in_specs=[in_smem()] + [in_vmem()] * (1 + len(extra)),
             out_specs=[in_vmem()] * len(CHUNKS),
             compiler_params=params,
             cost_estimate=pl.CostEstimate(flops=0, bytes_accessed=4 << 20, transcendentals=0),
-        )(meta, tile)
-
-    above = [shifted(part, "row", 1) for part in strips(meta_own)]
-    below = [shifted(part, "row", -1) for part in strips(meta_far)]
-    targets = [
-        shifted(measured[at : at + size], "row", 1) for at, size in zip(starts, CHUNKS)
-    ]
+        )(meta, tile, *extra)
+
+    up_strips = strips(meta_own, measured)
+    meta_mid = shifted(lax.optimization_barrier((meta_own, up_strips[0]))[0], "row", 1)
+    down_strips = strips(meta_far)
+    above, below = [], []
+    for up, down in zip(up_strips, down_strips):
+        if above:
+            up, down, _, _ = lax.optimization_barrier((up, down, above[-1], below[-1]))
+        above.append(shifted(up, "row", 1))
+        below.append(shifted(down, "row", -1))
     prop = jnp.stack([jnp.cos(propagator_phase), jnp.sin(propagator_phase)])
-    tables = [jnp.asarray(table) for table in fourier_blocks(pixels)]
-
+    tables = jnp.asarray(fourier_tables(pixels))
+
+    share = pixels // peers
     total = jnp.zeros((2 * modes + 1, pixels, pixels), F32)
     mid, back_own, back_far = [], [], []
     for index, (first, size) in enumerate(zip(starts, CHUNKS)):
         strip = jax.ShapeDtypeStruct((size, planes, tile_rows, pixels), F32)
+        part = jax.ShapeDtypeStruct((peers // 2, 2 * modes + 1, share, pixels), F32)
+        shares = [part, part] if index == len(CHUNKS) - 1 else []
         field = pltpu.VMEM((BATCH, planes, pixels, pixels), F32)
         kept = pltpu.VMEM((BATCH, modes, 2, pixels, pixels), F32)
-        to_above, to_mid, to_below, total = pl.pallas_call(
+        to_above, to_mid, to_below, total, *shares = pl.pallas_call(
             functools.partial(slot_kernel, first),
-            out_shape=[strip, strip, strip, jax.ShapeDtypeStruct(total.shape, F32)],
-            in_specs=[in_smem()] + [in_vmem()] * 11,
-            out_specs=[in_vmem()] * 4,
-            scratch_shapes=[
-                pltpu.VMEM((planes, 3 * tile_rows, pixels), F32),
-                field,
-                field,
-                kept,
-                kept,
-            ],
+            out_shape=[strip, strip, strip, jax.ShapeDtypeStruct(total.shape, F32)] + shares,
+            in_specs=[in_smem()] + [in_vmem()] * 7,
+            out_specs=[in_vmem()] * (4 + len(shares)),
+            scratch_shapes=[pltpu.VMEM((planes, 3 * tile_rows, pixels), F32), field, field, kept, kept],
             compiler_params=params,
             cost_estimate=pl.CostEstimate(
                 flops=size * 6 * modes * 3 * 16 * pixels**3, bytes_accessed=8 << 20, transcendentals=0
             ),
-        )(meta_mid, tile, above[index], below[index], targets[index], probe_modes, prop, *tables, total)
+        )(meta_mid, tile, above[index], below[index], probe_modes, prop, tables, total)
         mid.append(to_mid)
         back_own.append(shifted(to_above, "row", -1))
         back_far.append(shifted(to_below, "row", 1))
 
+    own, other = shares
+    own, other, back_own[:-1], back_far[:-1] = lax.optimization_barrier(
+        (own, other, back_own[:-1], back_far[:-1])
+    )
+    both = own + lax.ppermute(other, "row", [(i, i ^ 1) for i in range(peers)])
+    parts = lax.all_to_all(
+        both, "row", 0, 0, axis_index_groups=[list(range(core, peers, 2)) for core in range(2)]
+    )
+    spread = pl.pallas_call(
+        step_kernel,
+        out_shape=jax.ShapeDtypeStruct((peers, 2 * modes, share, pixels), F32),
+        in_specs=[in_vmem()],
+        out_specs=in_vmem(),
+        compiler_params=params,
+    )(parts)
+    gathered = lax.all_to_all(spread, "row", 0, 0)
+
     object_grad = pl.pallas_call(
-        functools.partial(add_kernel, pixels, 3),
+        functools.partial(add_kernel, pixels),
         out_shape=jax.ShapeDtypeStruct(tile.shape, F32),
         in_specs=[in_smem()] * 3 + [in_vmem()] * (3 * len(CHUNKS)),
         out_specs=in_vmem(),
@@ -252,12 +304,13 @@
         cost_estimate=pl.CostEstimate(flops=0, bytes_accessed=5 << 20, transcendentals=0),
     )(meta_own, meta_mid, meta_far, *mid, *back_own, *back_far).reshape(object_slices.shape)
 
-    share = pixels // peers
-    sent = total.reshape(2 * modes + 1, peers, share, pixels).swapaxes(0, 1)
-    summed = lax.all_to_all(sent, "row", 0, 0).sum(axis=0)
-    step = summed[: 2 * modes] / (summed[2 * modes :] + 1.0)
-    spread = lax.all_to_all(jnp.broadcast_to(step, (peers,) + step.shape), "row", 0, 0)
-    probe_step = spread.swapaxes(0, 1).reshape(probe_modes.shape)
+    probe_step = pl.pallas_call(
+        order_kernel,
+        out_shape=jax.ShapeDtypeStruct((2 * modes, pixels, pixels), F32),
+        in_specs=[in_vmem()],
+        out_specs=in_vmem(),
+        compiler_params=params,
+    )(gathered).reshape(probe_modes.shape)
     return (object_grad, probe_step)
 
 

time: 141 us -> 127 us (0.901)
  the two profiles are of different devices: /device:TPU:1 before, /device:TPU:0 now
where the time goes in v3:
time: 127 us; the launch traced here: 125 us
  starting transfers between devices  56.8 us (45%)
  waiting for transfers between devices  24.1 us (19%)
  Pallas kernels  21.3 us (17%)
  blocking collectives  17.6 us (14%)
  local copies, waits for them, and re-layouts  3.69 us (3%)
  between operations  1.45 us (1%)
    ppermute x14, starting transfers between devices, shifted(): lax.ppermute(array, axis, [(i, (i + by) % peers) for i in range(peers)])  44.7 us
    ppermute x14, waiting for transfers between devices, shifted(): lax.ppermute(array, axis, [(i, (i + by) % peers) for i in range(peers)])  22.9 us
    all_to_all x1, blocking collectives, local(): lax.all_to_all(both, 'row', 0, 0, axis_index_groups=[list(range(core, pee...  17.6 us
    pallas_call x3, Pallas kernels, local(): pl.pallas_call(functools.partial(slot_kernel, first), out_shape=[strip, s...  14.2 us
    ppermute x1, starting transfers between devices, local(): both = own + lax.ppermute(other, 'row', [(i, i ^ 1) for i in range(peers)])  8.53 us
    all_to_all x1, starting transfers between devices, local(): gathered = lax.all_to_all(spread, 'row', 0, 0)  3.57 us
    unnamed x15, local copies, waits for them, and re-layouts  3.41 us
    pallas_call x1, Pallas kernels, local(): pl.pallas_call(functools.partial(add_kernel, pixels), out_shape=jax.Shape...  3.03 us
  transfers between devices with their start and end apart: 16, of which 6 were waited for; matrix products, arithmetic and copies ran while one was open for 0% of the time, Pallas kernels for 15%

profile of v3, /device:TPU:0, one launch (start us, length us, event | category | flops | bytes accessed | tf_op | source)
XLA Modules:
  0.0 125.0 jit_solution(1805062017177218344)
XLA Ops:
  0.6 0.8 copy.9
  2.0 0.0 copy-start
  2.1 1.6 %copy-done = f32[2,2,64,2048]{3,2,1,0:T(8,128)S(1)} copy-done((f32[2,2,64,2048]{3,2,1,0:T(8,128)S(1)}, f32[2,2,64,2048]{3,2,1,0:T(8,128)}, u32[]{:S(2)}) %copy-start) | copy-done | bytes 2097176
  3.6 1.0 copy-done.2
  4.7 1.2 shard_map.89
  5.9 0.0 copy-start.3
  5.9 0.0 copy-start.5
  5.9 0.5 collective-permute-start.2
  6.4 2.6 %collective-permute-start.1 = (s32[8,3]{1,0:T(8,128)S(1)}, s32[8,3]{1,0:T(8,128)S(1)}, u32[]{:S(2)}, u32[]{:S(2)}) collective-permute-start(s32[8,3]{1,0:T(8,128)S(1)} %concatenate.3.meta.meta_own), channel_id=1, source_target_pairs={{0,2},{1,3},{2,4},{3,5},{4,6},{5,7},{6,8},{7,9},{8,10},{9,11},{10,... | collective-permute-start | bytes 296 | tf_op jit(solution)/shard_map/ppermute | solution.py:20
  9.0 4.7 %collective-permute-done.1.meta.meta_far = s32[8,3]{1,0:T(8,128)S(1)} collective-permute-done((s32[8,3]{1,0:T(8,128)S(1)}, s32[8,3]{1,0:T(8,128)S(1)}, u32[]{:S(2)}, u32[]{:S(2)}) %collective-permute-start.1) | collective-permute-done | bytes 128 | tf_op jit(solution)/shard_map/ppermute | solution.py:20
  13.7 1.2 shard_map.90
  14.9 5.3 %collective-permute-start.3 = (f32[2,4,64,128]{3,2,1,0:T(8,128)S(1)}, f32[2,4,64,128]{3,2,1,0:T(8,128)S(1)}, u32[]{:S(2)}, u32[]{:S(2)}) collective-permute-start(f32[2,4,64,128]{3,2,1,0:T(8,128)S(1)} %get-tuple-element.34), channel_id=1, source_target_pairs={{0,15},{1,0},{2,1},{3,2},{4,3},{5,4},{6,5},{7,6},{8,7},{9,8},{10,9... | collective-permute-start | bytes 786440 | tf_op jit(solution)/shard_map/ppermute | solution.py:20
  20.2 0.0 collective-permute-start
  20.2 3.9 %collective-permute-done.3.below = f32[2,4,64,128]{3,2,1,0:T(8,128)S(1)} collective-permute-done((f32[2,4,64,128]{3,2,1,0:T(8,128)S(1)}, f32[2,4,64,128]{3,2,1,0:T(8,128)S(1)}, u32[]{:S(2)}, u32[]{:S(2)}) %collective-permute-start.3) | collective-permute-done | bytes 262176 | tf_op jit(solution)/shard_map/ppermute | solution.py:20
  24.1 0.0 collective-permute-done.2.above
  24.1 0.0 collective-permute-start.4
  24.1 0.2 cosine_bitcast_fusion
  24.4 4.7 %collective-permute-start.5 = (f32[4,4,64,128]{3,2,1,0:T(8,128)S(1)}, f32[4,4,64,128]{3,2,1,0:T(8,128)S(1)}, u32[]{:S(2)}, u32[]{:S(2)}) collective-permute-start(f32[4,4,64,128]{3,2,1,0:T(8,128)S(1)} %get-tuple-element.39), channel_id=1, source_target_pairs={{0,15},{1,0},{2,1},{3,2},{4,3},{5,4},{6,5},{7,6},{8,7},{9,8},{10,9... | collective-permute-start | bytes 1572872 | tf_op jit(solution)/shard_map/ppermute | solution.py:20
  29.1 0.0 collective-permute-done.meta.meta_mid
  29.2 9.7 %shard_map.91 = (f32[2,4,64,128]{3,2,1,0:T(8,128)S(1)}, f32[2,4,64,128]{3,2,1,0:T(8,128)S(1)}, f32[2,4,64,128]{3,2,1,0:T(8,128)S(1)}, f32[9,128,128]{2,1,0:T(8,128)S(1)}) custom-call(s32[8,3]{1,0:T(8,128)S(1)} %collective-permute-done.meta.meta_mid, f32[4,64,2048]{2,1,0:T(8,128)S(1)} %bitcast.13, f32[2,6,64,128]{3,2,1,0:T(8,128)S(1)} %collective-permute-done.2.above, ...), custom_call_target="tpu_custom_call" | custom-call | flops 4831838208 | bytes 8388608 | tf_op jit(solution)/shard_map/pallas_call | solution.py:266
  38.9 0.0 collective-permute-done.5.below
  38.9 0.0 collective-permute-done.4.above
  38.9 2.6 %collective-permute-start.6 = (f32[2,6,64,128]{3,2,1,0:T(8,128)S(1)}, f32[2,6,64,128]{3,2,1,0:T(8,128)S(1)}, u32[]{:S(2)}, u32[]{:S(2)}) collective-permute-start(f32[2,6,64,128]{3,2,1,0:T(8,128)S(1)} %get-tuple-element.44), channel_id=1, source_target_pairs={{0,1},{1,2},{2,3},{3,4},{4,5},{5,6},{6,7},{7,8},{8,9},{9,10},{10,1... | collective-permute-start | bytes 1179656 | tf_op jit(solution)/shard_map/ppermute | solution.py:20
  41.5 1.9 %collective-permute-start.7 = (f32[2,4,64,128]{3,2,1,0:T(8,128)S(1)}, f32[2,4,64,128]{3,2,1,0:T(8,128)S(1)}, u32[]{:S(2)}, u32[]{:S(2)}) collective-permute-start(f32[2,4,64,128]{3,2,1,0:T(8,128)S(1)} %get-tuple-element.45), channel_id=1, source_target_pairs={{0,15},{1,0},{2,1},{3,2},{4,3},{5,4},{6,5},{7,6},{8,7},{9,8},{10,9... | collective-permute-start | bytes 786440 | tf_op jit(solution)/shard_map/ppermute | solution.py:20
  43.4 1.8 %shard_map.92 = (f32[4,4,64,128]{3,2,1,0:T(8,128)S(1)}, f32[4,4,64,128]{3,2,1,0:T(8,128)S(1)}, f32[4,4,64,128]{3,2,1,0:T(8,128)S(1)}, f32[9,128,128]{2,1,0:T(8,128)S(1)}) custom-call(s32[8,3]{1,0:T(8,128)S(1)} %collective-permute-done.meta.meta_mid, f32[4,64,2048]{2,1,0:T(8,128)} %bitcast.9, f32[4,6,64,128]{3,2,1,0:T(8,128)S(1)} %collective-permute-done.4.above, ...), custom_call_target="tpu_custom_call" | custom-call | flops 9663676416 | bytes 8388608 | tf_op jit(solution)/shard_map/pallas_call | solution.py:266
  45.2 0.1 collective-permute-start.11
  45.3 4.4 %collective-permute-start.9 = (f32[4,4,64,128]{3,2,1,0:T(8,128)S(1)}, f32[4,4,64,128]{3,2,1,0:T(8,128)S(1)}, u32[]{:S(2)}, u32[]{:S(2)}) collective-permute-start(f32[4,4,64,128]{3,2,1,0:T(8,128)S(1)} %get-tuple-element.51), channel_id=1, source_target_pairs={{0,15},{1,0},{2,1},{3,2},{4,3},{5,4},{6,5},{7,6},{8,7},{9,8},{10,9... | collective-permute-start | bytes 1572872 | tf_op jit(solution)/shard_map/ppermute | solution.py:20
  49.7 13.5 %collective-permute-start.10 = (f32[2,4,64,128]{3,2,1,0:T(8,128)S(1)}, f32[2,4,64,128]{3,2,1,0:T(8,128)S(1)}, u32[]{:S(2)}, u32[]{:S(2)}) collective-permute-start(f32[2,4,64,128]{3,2,1,0:T(8,128)S(1)} %get-tuple-element.52), channel_id=1, source_target_pairs={{0,1},{1,2},{2,3},{3,4},{4,5},{5,6},{6,7},{7,8},{8,9},{9,10},{10,1... | collective-permute-start | bytes 786440 | tf_op jit(solution)/shard_map/ppermute | solution.py:20
  63.2 0.0 collective-permute-done.7.below
  63.2 4.7 %collective-permute-start.8 = (f32[2,4,64,128]{3,2,1,0:T(8,128)S(1)}, f32[2,4,64,128]{3,2,1,0:T(8,128)S(1)}, u32[]{:S(2)}, u32[]{:S(2)}) collective-permute-start(f32[2,4,64,128]{3,2,1,0:T(8,128)S(1)} %get-tuple-element.50), channel_id=1, source_target_pairs={{0,15},{1,0},{2,1},{3,2},{4,3},{5,4},{6,5},{7,6},{8,7},{9,8},{10,9... | collective-permute-start | bytes 786440 | tf_op jit(solution)/shard_map/ppermute | solution.py:20
  68.0 0.0 collective-permute-done.6.above
  68.0 2.7 %shard_map.93 = (f32[2,4,64,128]{3,2,1,0:T(8,128)S(1)}, f32[2,4,64,128]{3,2,1,0:T(8,128)S(1)}, f32[2,4,64,128]{3,2,1,0:T(8,128)S(1)}, f32[9,128,128]{2,1,0:T(8,1...) custom-call(s32[8,3]{1,0:T(8,128)S(1)} %collective-permute-done.meta.meta_mid, f32[4,64,2048]{2,1,0:T(8,128)} %bitcast.10, ...), custom_call_target="tpu_custom_call" | custom-call | flops 4831838208 | bytes 8388608 | tf_op jit(solution)/shard_map/pallas_call | solution.py:266
  70.6 1.5 %collective-permute-done.10.refs_6_ = f32[2,4,64,128]{3,2,1,0:T(8,128)S(1)} collective-permute-done((f32[2,4,64,128]{3,2,1,0:T(8,128)S(1)}, f32[2,4,64,128]{3,2,1,0:T(8,128)S(1)}, u32[]{:S(2)}, u32[]{:S(2)}) %collective-permute-start.10) | collective-permute-done | bytes 262176 | tf_op jit(solution)/shard_map/ppermute | solution.py:20
  72.1 0.0 collective-permute-done.8.refs_3_
  72.1 0.0 collective-permute-done.11.refs_7_
  72.1 0.0 collective-permute-done.9.refs_4_
  72.1 8.5 %collective-permute-start.14 = (f32[8,9,8,128]{3,2,1,0:T(8,128)S(1)}, f32[8,9,8,128]{3,2,1,0:T(8,128)S(1)}, u32[]{:S(2)}, u32[]{:S(2)}) collective-permute-start(f32[8,9,8,128]{3,2,1,0:T(8,128)S(1)} %get-tuple-element.61), channel_id=1, source_target_pairs={{0,1},{1,0},{2,3},{3,2},{4,5},{5,4},{6,7},{7,6},{8,9},{9,8},{10,11... | collective-permute-start | bytes 884744 | tf_op jit(solution)/shard_map/ppermute | solution.py:285
  80.7 1.2 collective-permute-done.14
  81.9 17.6 %all_to_all.10.parts = f32[8,9,8,128]{3,2,1,0:T(8,128)S(1)} all-to-all(f32[8,9,8,128]{3,2,1,0:T(8,128)S(1)} %add.5), channel_id=1, replica_groups={{0,2,4,6,8,10,12,14},{1,3,5,7,9,11,13,15},{16,18,20,22,24,26,28,30},{17..., dimensions={0} | all-to-all | bytes 589824 | tf_op jit(solution)/shard_map/all_to_all | solution.py:286
  99.5 0.9 shard_map.95
  100.3 3.6 %all-to-all-start.1 = ((f32[16,8,8,128]{3,2,1,0:T(8,128)}), f32[16,8,8,128]{3,2,1,0:T(8,128)S(1)}, u32[]{:S(2)}, u32[]{:S(2)}) async-start(f32[16,8,8,128]{3,2,1,0:T(8,128)} %shard_map.95), calls=%async_computation.1 | async-start | bytes 1048576 | tf_op jit(solution)/shard_map/all_to_all | solution.py:296
  103.9 4.3 %collective-permute-start.12 = (f32[2,4,64,128]{3,2,1,0:T(8,128)}, f32[2,4,64,128]{3,2,1,0:T(8,128)S(1)}, u32[]{:S(2)}, u32[]{:S(2)}) collective-permute-start(f32[2,4,64,128]{3,2,1,0:T(8,128)} %copy-done.4), channel_id=1, source_target_pairs={{0,15},{1,0},{2,1},{3,2},{4,3},{5,4},{6,5},{7,6},{8,7},{9,8},{10,9... | collective-permute-start | bytes 786440 | tf_op jit(solution)/shard_map/ppermute | solution.py:20
  108.3 0.0 collective-permute-start.13
  108.3 8.0 %collective-permute-done.12.refs_5_ = f32[2,4,64,128]{3,2,1,0:T(8,128)S(1)} collective-permute-done((f32[2,4,64,128]{3,2,1,0:T(8,128)}, f32[2,4,64,128]{3,2,1,0:T(8,128)S(1)}, u32[]{:S(2)}, u32[]{:S(2)}) %collective-permute-start.12) | collective-permute-done | bytes 262176 | tf_op jit(solution)/shard_map/ppermute | solution.py:20
  116.2 4.9 %collective-permute-done.13.refs_8_ = f32[2,4,64,128]{3,2,1,0:T(8,128)S(1)} collective-permute-done((f32[2,4,64,128]{3,2,1,0:T(8,128)S(1)}, f32[2,4,64,128]{3,2,1,0:T(8,128)S(1)}, u32[]{:S(2)}, u32[]{:S(2)}) %collective-permute-start.13) | collective-permute-done | bytes 262176 | tf_op jit(solution)/shard_map/ppermute | solution.py:20
  121.1 3.0 %shard_map.94 = f32[4,64,2048]{2,1,0:T(8,128)} custom-call(s32[8,3]{1,0:T(8,128)S(1)} %concatenate.3.meta.meta_own, s32[8,3]{1,0:T(8,128)S(1)} %collective-permute-done.meta.meta_mid, s32[8,3]{1,0:T(8,128)S(1)} %collective-permute-done.1.meta.meta_far, f32[2,4,64,128]{3,2,1,0:T(8,128)S(1)} %get-tuple-element.35.refs_0_, ...), custom_call_target="tpu_custom_call" | custom-call | bytes 5242880 | tf_op jit(solution)/shard_map/pallas_call | solution.py:298
  124.2 0.0 all-to-all-done.1.parts
  124.2 0.8 shard_map.96
  (13 shorter events, 0.1 us)
Async XLA Ops:
  2.0 1.6 %copy-start = (f32[2,2,64,2048]{3,2,1,0:T(8,128)S(1)}, f32[2,2,64,2048]{3,2,1,0:T(8,128)}, u32[]{:S(2)}) copy-start(f32[2,2,64,2048]{3,2,1,0:T(8,128)} %param.7) | copy-start | bytes 6291460
  3.6 1.0 copy-start.2
  4.7 9.0 %copy-start.1 = (f32[2,2,64,2048]{3,2,1,0:T(8,128)S(1)}, f32[2,2,64,2048]{3,2,1,0:T(8,128)}, u32[]{:S(2)}) copy-start(f32[2,2,64,2048]{3,2,1,0:T(8,128)} %param.7) | copy-start | bytes 6291460
  4.7 19.5 %copy-start.6 = (f32[128,128]{1,0:T(8,128)S(1)}, f32[128,128]{1,0:T(8,128)}, u32[]{:S(2)}) copy-start(f32[128,128]{1,0:T(8,128)} %param.9) | copy-start | bytes 196612
  5.9 23.3 %copy-start.3 = (f32[4,2,128,128]{3,2,1,0:T(8,128)S(1)}, f32[4,2,128,128]{3,2,1,0:T(8,128)}, u32[]{:S(2)}) copy-start(f32[4,2,128,128]{3,2,1,0:T(8,128)} %probe.5) | copy-start | bytes 1572868
  5.9 23.3 %copy-start.5 = (bf16[4,256,256]{2,1,0:T(8,128)(2,1)S(1)}, bf16[4,256,256]{2,1,0:T(8,128)(2,1)}, u32[]{:S(2)}) copy-start(bf16[4,256,256]{2,1,0:T(8,128)(2,1)} %constant.4.clone.tables) | copy-start | bytes 1572868
  5.9 18.2 %collective-permute-start.2 = (f32[2,6,64,128]{3,2,1,0:T(8,128)S(1)}, f32[2,6,64,128]{3,2,1,0:T(8,128)S(1)}, u32[]{:S(2)}, u32[]{:S(2)}) collective-permute-start(f32[2,6,64,128]{3,2,1,0:T(8,128)S(1)} %get-tuple-element.32), channel_id=1, source_target_pairs={{0,1},{1,2},{2,3},{3,4},{4,5},{5,6},{6,7},{7,8},{8,9},{9,10},{10,1... | collective-permute-start | bytes 1179656 | tf_op jit(solution)/shard_map/ppermute | solution.py:20
  6.4 7.2 %collective-permute-start.1 = (s32[8,3]{1,0:T(8,128)S(1)}, s32[8,3]{1,0:T(8,128)S(1)}, u32[]{:S(2)}, u32[]{:S(2)}) collective-permute-start(s32[8,3]{1,0:T(8,128)S(1)} %concatenate.3.meta.meta_own), channel_id=1, source_target_pairs={{0,2},{1,3},{2,4},{3,5},{4,6},{5,7},{6,8},{7,9},{8,10},{9,11},{10,... | collective-permute-start | bytes 296 | tf_op jit(solution)/shard_map/ppermute | solution.py:20
  14.9 9.2 %collective-permute-start.3 = (f32[2,4,64,128]{3,2,1,0:T(8,128)S(1)}, f32[2,4,64,128]{3,2,1,0:T(8,128)S(1)}, u32[]{:S(2)}, u32[]{:S(2)}) collective-permute-start(f32[2,4,64,128]{3,2,1,0:T(8,128)S(1)} %get-tuple-element.34), channel_id=1, source_target_pairs={{0,15},{1,0},{2,1},{3,2},{4,3},{5,4},{6,5},{7,6},{8,7},{9,8},{10,9... | collective-permute-start | bytes 786440 | tf_op jit(solution)/shard_map/ppermute | solution.py:20
  20.2 8.9 %collective-permute-start = (s32[8,3]{1,0:T(8,128)S(1)}, s32[8,3]{1,0:T(8,128)S(1)}, u32[]{:S(2)}, u32[]{:S(2)}) collective-permute-start(s32[8,3]{1,0:T(8,128)S(1)} %concatenate.3.meta.meta_own), channel_id=1, source_target_pairs={{0,1},{1,2},{2,3},{3,4},{4,5},{5,6},{6,7},{7,8},{8,9},{9,10},{10,1... | collective-permute-start | bytes 296 | tf_op jit(solution)/shard_map/ppermute | solution.py:20
  24.1 14.8 %collective-permute-start.4 = (f32[4,6,64,128]{3,2,1,0:T(8,128)S(1)}, f32[4,6,64,128]{3,2,1,0:T(8,128)S(1)}, u32[]{:S(2)}, u32[]{:S(2)}) collective-permute-start(f32[4,6,64,128]{3,2,1,0:T(8,128)S(1)} %get-tuple-element.38), channel_id=1, source_target_pairs={{0,1},{1,2},{2,3},{3,4},{4,5},{5,6},{6,7},{7,8},{8,9},{9,10},{10,1... | collective-permute-start | bytes 2359304 | tf_op jit(solution)/shard_map/ppermute | solution.py:20
  24.4 14.5 %collective-permute-start.5 = (f32[4,4,64,128]{3,2,1,0:T(8,128)S(1)}, f32[4,4,64,128]{3,2,1,0:T(8,128)S(1)}, u32[]{:S(2)}, u32[]{:S(2)}) collective-permute-start(f32[4,4,64,128]{3,2,1,0:T(8,128)S(1)} %get-tuple-element.39), channel_id=1, source_target_pairs={{0,15},{1,0},{2,1},{3,2},{4,3},{5,4},{6,5},{7,6},{8,7},{9,8},{10,9... | collective-permute-start | bytes 1572872 | tf_op jit(solution)/shard_map/ppermute | solution.py:20
  38.9 29.0 %collective-permute-start.6 = (f32[2,6,64,128]{3,2,1,0:T(8,128)S(1)}, f32[2,6,64,128]{3,2,1,0:T(8,128)S(1)}, u32[]{:S(2)}, u32[]{:S(2)}) collective-permute-start(f32[2,6,64,128]{3,2,1,0:T(8,128)S(1)} %get-tuple-element.44), channel_id=1, source_target_pairs={{0,1},{1,2},{2,3},{3,4},{4,5},{5,6},{6,7},{7,8},{8,9},{9,10},{10,1... | collective-permute-start | bytes 1179656 | tf_op jit(solution)/shard_map/ppermute | solution.py:20
  41.5 21.7 %collective-permute-start.7 = (f32[2,4,64,128]{3,2,1,0:T(8,128)S(1)}, f32[2,4,64,128]{3,2,1,0:T(8,128)S(1)}, u32[]{:S(2)}, u32[]{:S(2)}) collective-permute-start(f32[2,4,64,128]{3,2,1,0:T(8,128)S(1)} %get-tuple-element.45), channel_id=1, source_target_pairs={{0,15},{1,0},{2,1},{3,2},{4,3},{5,4},{6,5},{7,6},{8,7},{9,8},{10,9... | collective-permute-start | bytes 786440 | tf_op jit(solution)/shard_map/ppermute | solution.py:20
  45.2 26.9 %collective-permute-start.11 = (f32[4,4,64,128]{3,2,1,0:T(8,128)S(1)}, f32[4,4,64,128]{3,2,1,0:T(8,128)S(1)}, u32[]{:S(2)}, u32[]{:S(2)}) collective-permute-start(f32[4,4,64,128]{3,2,1,0:T(8,128)S(1)} %get-tuple-element.53), channel_id=1, source_target_pairs={{0,1},{1,2},{2,3},{3,4},{4,5},{5,6},{6,7},{7,8},{8,9},{9,10},{10,1... | collective-permute-start | bytes 1572872 | tf_op jit(solution)/shard_map/ppermute | solution.py:20
  45.3 26.8 %collective-permute-start.9 = (f32[4,4,64,128]{3,2,1,0:T(8,128)S(1)}, f32[4,4,64,128]{3,2,1,0:T(8,128)S(1)}, u32[]{:S(2)}, u32[]{:S(2)}) collective-permute-start(f32[4,4,64,128]{3,2,1,0:T(8,128)S(1)} %get-tuple-element.51), channel_id=1, source_target_pairs={{0,15},{1,0},{2,1},{3,2},{4,3},{5,4},{6,5},{7,6},{8,7},{9,8},{10,9... | collective-permute-start | bytes 1572872 | tf_op jit(solution)/shard_map/ppermute | solution.py:20
  49.7 22.4 %collective-permute-start.10 = (f32[2,4,64,128]{3,2,1,0:T(8,128)S(1)}, f32[2,4,64,128]{3,2,1,0:T(8,128)S(1)}, u32[]{:S(2)}, u32[]{:S(2)}) collective-permute-start(f32[2,4,64,128]{3,2,1,0:T(8,128)S(1)} %get-tuple-element.52), channel_id=1, source_target_pairs={{0,1},{1,2},{2,3},{3,4},{4,5},{5,6},{6,7},{7,8},{8,9},{9,10},{10,1... | collective-permute-start | bytes 786440 | tf_op jit(solution)/shard_map/ppermute | solution.py:20
  63.2 8.9 %collective-permute-start.8 = (f32[2,4,64,128]{3,2,1,0:T(8,128)S(1)}, f32[2,4,64,128]{3,2,1,0:T(8,128)S(1)}, u32[]{:S(2)}, u32[]{:S(2)}) collective-permute-start(f32[2,4,64,128]{3,2,1,0:T(8,128)S(1)} %get-tuple-element.50), channel_id=1, source_target_pairs={{0,15},{1,0},{2,1},{3,2},{4,3},{5,4},{6,5},{7,6},{8,7},{9,8},{10,9... | collective-permute-start | bytes 786440 | tf_op jit(solution)/shard_map/ppermute | solution.py:20
  70.6 11.3 %copy-start.4 = (f32[2,4,64,128]{3,2,1,0:T(8,128)}, f32[2,4,64,128]{3,2,1,0:T(8,128)S(1)}, u32[]{:S(2)}) copy-start(f32[2,4,64,128]{3,2,1,0:T(8,128)S(1)} %get-tuple-element.56) | copy-start | bytes 786436
  72.1 9.7 %collective-permute-start.14 = (f32[8,9,8,128]{3,2,1,0:T(8,128)S(1)}, f32[8,9,8,128]{3,2,1,0:T(8,128)S(1)}, u32[]{:S(2)}, u32[]{:S(2)}) collective-permute-start(f32[8,9,8,128]{3,2,1,0:T(8,128)S(1)} %get-tuple-element.61), channel_id=1, source_target_pairs={{0,1},{1,0},{2,3},{3,2},{4,5},{5,4},{6,7},{7,6},{8,9},{9,8},{10,11... | collective-permute-start | bytes 884744 | tf_op jit(solution)/shard_map/ppermute | solution.py:285
  100.3 23.8 %all-to-all-start.1 = ((f32[16,8,8,128]{3,2,1,0:T(8,128)}), f32[16,8,8,128]{3,2,1,0:T(8,128)S(1)}, u32[]{:S(2)}, u32[]{:S(2)}) async-start(f32[16,8,8,128]{3,2,1,0:T(8,128)} %shard_map.95), calls=%async_computation.1 | async-start | bytes 1048576 | tf_op jit(solution)/shard_map/all_to_all | solution.py:296
  103.9 12.3 %collective-permute-start.12 = (f32[2,4,64,128]{3,2,1,0:T(8,128)}, f32[2,4,64,128]{3,2,1,0:T(8,128)S(1)}, u32[]{:S(2)}, u32[]{:S(2)}) collective-permute-start(f32[2,4,64,128]{3,2,1,0:T(8,128)} %copy-done.4), channel_id=1, source_target_pairs={{0,15},{1,0},{2,1},{3,2},{4,3},{5,4},{6,5},{7,6},{8,7},{9,8},{10,9... | collective-permute-start | bytes 786440 | tf_op jit(solution)/shard_map/ppermute | solution.py:20
  108.3 12.9 %collective-permute-start.13 = (f32[2,4,64,128]{3,2,1,0:T(8,128)S(1)}, f32[2,4,64,128]{3,2,1,0:T(8,128)S(1)}, u32[]{:S(2)}, u32[]{:S(2)}) collective-permute-start(f32[2,4,64,128]{3,2,1,0:T(8,128)S(1)} %get-tuple-element.59), channel_id=1, source_target_pairs={{0,1},{1,2},{2,3},{3,4},{4,5},{5,6},{6,7},{7,8},{8,9},{9,10},{10,1... | collective-permute-start | bytes 786440 | tf_op jit(solution)/shard_map/ppermute | solution.py:20

commit v4 on v3

--- a/solution.py
+++ b/solution.py
@@ -78,49 +78,42 @@
     return turned[:, :pixels].reshape(-1, rows, pixels)
 
 
-def cut_kernel(pixels, extra, meta, tile, *refs):
-    if extra:
-        measured, *outs = refs
-    else:
-        outs = refs
+def cut_kernel(pixels, chunks, own, far, counts, tile, measured, *outs):
     planes, rows, _ = tile.shape
-    slot = 0
-    for out in outs:
-        for at in range(out.shape[0]):
-            out[at, :planes] = cut(tile, meta[slot, 1], pixels)
-            if extra:
-                out[at, planes:] = measured[slot].reshape(-1, rows, pixels)
-            slot += 1
-
-
-def add_kernel(pixels, meta_own, meta_mid, meta_far, *refs):
-    refs = list(refs)
-    out = refs.pop()
+    for (first, size), up, down in zip(chunks, outs[::2], outs[1::2]):
+        for at in range(size):
+            slot = first + at
+            up[at, :planes] = cut(tile, own[slot, 1], pixels)
+            live = jnp.where(slot < counts[0], 1.0, 0.0).astype(F32)
+            up[at, planes:] = (measured[slot] * live).reshape(-1, rows, pixels)
+            down[at] = cut(tile, far[slot, 1], pixels)
+
+
+def add_kernel(pixels, own, mid, far, *refs):
+    *refs, out = refs
     out[...] = jnp.zeros_like(out)
     count = len(refs) // 3
-    for meta, group in (
-        (meta_mid, refs[:count]),
-        (meta_own, refs[count : 2 * count]),
-        (meta_far, refs[2 * count :]),
-    ):
+    lane = lax.broadcasted_iota(jnp.int32, (1, 1, pixels), 2)
+    for offsets, group in ((mid, refs[:count]), (own, refs[count : 2 * count]), (far, refs[2 * count :])):
         first = 0
         for parts in group:
-            size = parts.shape[0]
-
-            def add(at, carry, parts=parts, first=first, meta=meta):
-                base, shift = place(meta[first + at, 1], out.shape[-1], pixels)
+
+            def add(at, carry, parts=parts, first=first, offsets=offsets):
+                base, shift = place(offsets[first + at, 1], out.shape[-1], pixels)
                 part = parts[at]
-                wide = jnp.concatenate([part, jnp.zeros_like(part)], axis=2)
-                turned = pltpu.roll(wide.reshape(-1, 2 * pixels), shift, 1).reshape(wide.shape)
-                out[:, :, pl.ds(base, 2 * pixels)] += turned
+                turned = pltpu.roll(part.reshape(-1, pixels), lax.rem(shift, pixels), 1).reshape(part.shape)
+                out[:, :, pl.ds(base, pixels)] += jnp.where(lane >= shift, turned, 0.0)
+                out[:, :, pl.ds(pl.multiple_of(base + pixels, pixels), pixels)] += jnp.where(
+                    lane < shift, turned, 0.0
+                )
                 return carry
 
-            lax.fori_loop(0, jnp.clip(meta[0, 2] - first, 0, size), add, 0)
-            first += size
+            lax.fori_loop(0, parts.shape[0], add, 0)
+            first += parts.shape[0]
 
 
 def slot_kernel(
-    first, meta, tile, above, below, probe, prop, tables, so_far,
+    first, offsets, tile, above, below, probe, prop, tables, so_far,
     out_above, out_mid, out_below, total, *refs,
 ):
     shares, (window, patch, grads, exit_wave, far) = refs[:-5], refs[-5:]
@@ -130,15 +123,21 @@
     rows = above.shape[2]
     total[...] = so_far[...]
     held = [(s, m) for s in range(BATCH) for m in range(modes)]
-    live_slots = jnp.clip(meta[0, 2] - first, 0, size)
-
-    def visit(step, carry):
-        slots = [step * BATCH + s for s in range(BATCH)]
-        starts = [lax.rem(meta[first + at, 0], rows) for at in slots]
-        live = [jnp.where(at < live_slots, 1.0, 0.0).astype(F32) for at in slots]
+
+    def is_live(at):
+        return jnp.max(above[at, planes, :8]) > 0.0
+
+    def leave(slots):
+        for at in slots:
+            for out in (out_above, out_mid, out_below):
+                out[at] = jnp.zeros(out.shape[1:], F32)
+
+    def visit(slots):
+        starts = [lax.rem(offsets[first + at, 0], rows) for at in slots]
+        live = [jnp.where(is_live(at), 1.0, 0.0).astype(F32) for at in slots]
         for s, at in enumerate(slots):
             window[:, :rows] = above[at, :planes]
-            window[:, rows : 2 * rows] = cut(tile, meta[first + at, 1], pixels)
+            window[:, rows : 2 * rows] = cut(tile, offsets[first + at, 1], pixels)
             window[:, 2 * rows :] = below[at]
             patch[s] = window[:, pl.ds(starts[s], pixels), :]
             total[2 * modes] += live[s] * (patch[s, 0] * patch[s, 0] + patch[s, 1] * patch[s, 1])
@@ -179,14 +178,20 @@
             out_above[at] = window[:, :rows]
             out_mid[at] = window[:, rows : 2 * rows]
             out_below[at] = window[:, 2 * rows :]
+
+    def step(index, carry):
+        slots = [index * BATCH + s for s in range(BATCH)]
+        some = is_live(slots[0])
+        pl.when(some)(lambda: visit(slots))
+        pl.when(jnp.logical_not(some))(lambda: leave(slots))
         return carry
 
-    lax.fori_loop(0, (live_slots + BATCH - 1) // BATCH, visit, 0)
+    lax.fori_loop(0, size // BATCH, step, 0)
 
     if shares:
         own, other = shares
         chips, _, share, _ = own.shape
-        core = lax.rem(meta[0, 0] // rows + 1, 2)
+        core = lax.rem(offsets[0, 0] // rows + 1, 2)
         for chip in range(chips):
             for plane in range(2 * modes + 1):
                 own[chip, plane] = total[plane, pl.ds((2 * chip + core) * share, share)]
@@ -219,34 +224,33 @@
 def local(object_slices, probe_modes, propagator_phase, measured, offsets, counts):
     slices, _, tile_rows, columns = object_slices.shape
     modes, _, pixels, _ = probe_modes.shape
-    slots = measured.shape[0]
     planes = 2 * slices
     peers = lax.axis_size("row")
     params = pltpu.CompilerParams(vmem_limit_bytes=VMEM_LIMIT)
     tile = object_slices.reshape(planes, tile_rows, columns)
     starts = [sum(CHUNKS[:i]) for i in range(len(CHUNKS))]
 
-    meta_own = jnp.concatenate([offsets, jnp.broadcast_to(counts, (slots, 1))], axis=1)
-    meta_far = shifted(meta_own, "row", 2)
-
-    def strips(meta, *extra):
-        rest = sum(part.size // (slots * tile_rows * pixels) for part in extra)
-        return pl.pallas_call(
-            functools.partial(cut_kernel, pixels, bool(extra)),
-            out_shape=[
-                jax.ShapeDtypeStruct((size, planes + rest, tile_rows, pixels), F32) for size in CHUNKS
-            ],
-            in_specs=[in_smem()] + [in_vmem()] * (1 + len(extra)),
-            out_specs=[in_vmem()] * len(CHUNKS),
+    far = shifted(offsets, "row", 2)
+    middle = shifted(offsets, "row", 1)
+
+    def strips(chunks):
+        shapes = []
+        for _, size in chunks:
+            for count in (planes + pixels // tile_rows, planes):
+                shapes.append(jax.ShapeDtypeStruct((size, count, tile_rows, pixels), F32))
+        outs = pl.pallas_call(
+            functools.partial(cut_kernel, pixels, chunks),
+            out_shape=shapes,
+            in_specs=[in_smem()] * 3 + [in_vmem()] * 2,
+            out_specs=[in_vmem()] * len(shapes),
             compiler_params=params,
             cost_estimate=pl.CostEstimate(flops=0, bytes_accessed=4 << 20, transcendentals=0),
-        )(meta, tile, *extra)
-
-    up_strips = strips(meta_own, measured)
-    meta_mid = shifted(lax.optimization_barrier((meta_own, up_strips[0]))[0], "row", 1)
-    down_strips = strips(meta_far)
+        )(offsets, far, counts, tile, measured)
+        return list(zip(outs[::2], outs[1::2]))
+
+    chunks = list(zip(starts, CHUNKS))
     above, below = [], []
-    for up, down in zip(up_strips, down_strips):
+    for up, down in strips(chunks[:1]) + strips(chunks[1:]):
         if above:
             up, down, _, _ = lax.optimization_barrier((up, down, above[-1], below[-1]))
         above.append(shifted(up, "row", 1))
@@ -273,7 +277,7 @@
             cost_estimate=pl.CostEstimate(
                 flops=size * 6 * modes * 3 * 16 * pixels**3, bytes_accessed=8 << 20, transcendentals=0
             ),
-        )(meta_mid, tile, above[index], below[index], probe_modes, prop, tables, total)
+        )(middle, tile, above[index], below[index], probe_modes, prop, tables, total)
         mid.append(to_mid)
         back_own.append(shifted(to_above, "row", -1))
         back_far.append(shifted(to_below, "row", 1))
@@ -283,6 +287,7 @@
         (own, other, back_own[:-1], back_far[:-1])
     )
     both = own + lax.ppermute(other, "row", [(i, i ^ 1) for i in range(peers)])
+    both, back_own, back_far = lax.optimization_barrier((both, back_own, back_far))
     parts = lax.all_to_all(
         both, "row", 0, 0, axis_index_groups=[list(range(core, peers, 2)) for core in range(2)]
     )
@@ -302,7 +307,7 @@
         out_specs=in_vmem(),
         compiler_params=params,
         cost_estimate=pl.CostEstimate(flops=0, bytes_accessed=5 << 20, transcendentals=0),
-    )(meta_own, meta_mid, meta_far, *mid, *back_own, *back_far).reshape(object_slices.shape)
+    )(offsets, middle, far, *mid, *back_own, *back_far).reshape(object_slices.shape)
 
     probe_step = pl.pallas_call(
         order_kernel,

time: 127 us -> 125 us (0.984)
  the two profiles are of different devices: /device:TPU:0 before, /device:TPU:1 now
where the time goes in v4:
time: 125 us; the launch traced here: 124 us
  Pallas kernels  51.4 us (41%)
  waiting for transfers between devices  30.8 us (25%)
  starting transfers between devices  23.5 us (19%)
  blocking collectives  11.7 us (9%)
  local copies, waits for them, and re-layouts  5.34 us (4%)
  between operations  1.43 us (1%)
    pallas_call x3, Pallas kernels, local(): pl.pallas_call(functools.partial(slot_kernel, first), out_shape=[strip, s...  41.6 us
    ppermute x14, waiting for transfers between devices, shifted(): lax.ppermute(array, axis, [(i, (i + by) % peers) for i in range(peers)])  23.2 us
    ppermute x14, starting transfers between devices, shifted(): lax.ppermute(array, axis, [(i, (i + by) % peers) for i in range(peers)])  16.5 us
    all_to_all x1, blocking collectives, local(): lax.all_to_all(both, 'row', 0, 0, axis_index_groups=[list(range(core, pee...  11.7 us
    all_to_all x1, waiting for transfers between devices, local(): gathered = lax.all_to_all(spread, 'row', 0, 0)  7.68 us
    all_to_all x1, starting transfers between devices, local(): gathered = lax.all_to_all(spread, 'row', 0, 0)  7.03 us
    pallas_call x1, Pallas kernels, local(): pl.pallas_call(functools.partial(add_kernel, pixels), out_shape=jax.Shape...  5.52 us
    unnamed x17, local copies, waits for them, and re-layouts  5.06 us
  transfers between devices with their start and end apart: 16, of which 9 were waited for; matrix products, arithmetic and copies ran while one was open for 0% of the time, Pallas kernels for 39%

profile of v4, /device:TPU:1, one launch (start us, length us, event | category | flops | bytes accessed | tf_op | source)
XLA Modules:
  0.0 124.2 jit_solution(10858140655931022904)
XLA Ops:
  0.6 0.8 copy.13.own
  1.4 2.1 %collective-permute-start.1 = (s32[8,2]{1,0:T(8,128)S(1)}, s32[8,2]{1,0:T(8,128)S(1)}, u32[]{:S(2)}, u32[]{:S(2)}) collective-permute-start(s32[8,2]{1,0:T(8,128)S(1)} %copy.13.own), channel_id=1, source_target_pairs={{0,2},{1,3},{2,4},{3,5},{4,6},{5,7},{6,8},{7,9},{8,10},{9,11},{10,... | collective-permute-start | bytes 200 | tf_op jit(solution)/shard_map/ppermute | solution.py:20
  4.1 3.4 %collective-permute-done.1.far = s32[8,2]{1,0:T(8,128)S(1)} collective-permute-done((s32[8,2]{1,0:T(8,128)S(1)}, s32[8,2]{1,0:T(8,128)S(1)}, u32[]{:S(2)}, u32[]{:S(2)}) %collective-permute-start.1) | collective-permute-done | bytes 96 | tf_op jit(solution)/shard_map/ppermute | solution.py:20
  7.5 1.6 %copy-done = f32[2,2,64,2048]{3,2,1,0:T(8,128)S(1)} copy-done((f32[2,2,64,2048]{3,2,1,0:T(8,128)S(1)}, f32[2,2,64,2048]{3,2,1,0:T(8,128)}, u32[]{:S(2)}) %copy-start) | copy-done | bytes 2097176
  9.1 1.0 copy-done.2
  10.1 1.0 shard_map.86
  11.1 0.0 copy-start.1
  11.1 0.0 copy-start.5
  11.2 0.0 copy-start.6
  11.2 0.2 collective-permute-start.2
  11.4 1.5 %collective-permute-start.3 = (f32[2,4,64,128]{3,2,1,0:T(8,128)S(1)}, f32[2,4,64,128]{3,2,1,0:T(8,128)S(1)}, u32[]{:S(2)}, u32[]{:S(2)}) collective-permute-start(f32[2,4,64,128]{3,2,1,0:T(8,128)S(1)} %get-tuple-element.39), channel_id=1, source_target_pairs={{0,15},{1,0},{2,1},{3,2},{4,3},{5,4},{6,5},{7,6},{8,7},{9,8},{10,9... | collective-permute-start | bytes 786440 | tf_op jit(solution)/shard_map/ppermute | solution.py:20
  12.8 0.3 collective-permute-start
  13.1 1.6 %shard_map.88 = (f32[4,6,64,128]{3,2,1,0:T(8,128)S(1)}, f32[4,4,64,128]{3,2,1,0:T(8,128)S(1)}, f32[2,6,64,128]{3,2,1,0:T(8,128)S(1)}, f32[2,4,64,128]{3,2,1,0:T(8,128)S(1)}) custom-call(s32[8,2]{1,0:T(8,128)S(1)} %copy.13.own, s32[8,2]{1,0:T(8,128)S(1)} %collective-permute-done.1.far, s32[1]{0:T(128)S(6)} %copy.14.counts, f32[4,64,2048]{2,1,0:T(8,128)S(1)} %bitcast.10, ...), custom_call_target="tpu_custom_call" | custom-call | bytes 4194304 | tf_op jit(solution)/shard_map/pallas_call | solution.py:241
  14.7 2.5 %collective-permute-done.3.below = f32[2,4,64,128]{3,2,1,0:T(8,128)S(1)} collective-permute-done((f32[2,4,64,128]{3,2,1,0:T(8,128)S(1)}, f32[2,4,64,128]{3,2,1,0:T(8,128)S(1)}, u32[]{:S(2)}, u32[]{:S(2)}) %collective-permute-start.3) | collective-permute-done | bytes 262176 | tf_op jit(solution)/shard_map/ppermute | solution.py:20
  17.2 1.7 %collective-permute-done.2.above = f32[2,6,64,128]{3,2,1,0:T(8,128)S(1)} collective-permute-done((f32[2,6,64,128]{3,2,1,0:T(8,128)S(1)}, f32[2,6,64,128]{3,2,1,0:T(8,128)S(1)}, u32[]{:S(2)}, u32[]{:S(2)}) %collective-permute-start.2) | collective-permute-done | bytes 393248 | tf_op jit(solution)/shard_map/ppermute | solution.py:20
  18.9 2.5 %collective-permute-start.4 = (f32[4,6,64,128]{3,2,1,0:T(8,128)S(1)}, f32[4,6,64,128]{3,2,1,0:T(8,128)S(1)}, u32[]{:S(2)}, u32[]{:S(2)}) collective-permute-start(f32[4,6,64,128]{3,2,1,0:T(8,128)S(1)} %get-tuple-element.43), channel_id=1, source_target_pairs={{0,1},{1,2},{2,3},{3,4},{4,5},{5,6},{6,7},{7,8},{8,9},{9,10},{10,1... | collective-permute-start | bytes 2359304 | tf_op jit(solution)/shard_map/ppermute | solution.py:20
  21.4 0.2 cosine_bitcast_fusion
  21.6 1.4 %collective-permute-start.5 = (f32[4,4,64,128]{3,2,1,0:T(8,128)S(1)}, f32[4,4,64,128]{3,2,1,0:T(8,128)S(1)}, u32[]{:S(2)}, u32[]{:S(2)}) collective-permute-start(f32[4,4,64,128]{3,2,1,0:T(8,128)S(1)} %get-tuple-element.44), channel_id=1, source_target_pairs={{0,15},{1,0},{2,1},{3,2},{4,3},{5,4},{6,5},{7,6},{8,7},{9,8},{10,9... | collective-permute-start | bytes 1572872 | tf_op jit(solution)/shard_map/ppermute | solution.py:20
  23.0 0.0 collective-permute-done.offsets.mid
  23.1 9.8 %shard_map.87 = (f32[2,4,64,128]{3,2,1,0:T(8,128)S(1)}, f32[2,4,64,128]{3,2,1,0:T(8,128)S(1)}, f32[2,4,64,128]{3,2,1,0:T(8,128)S(1)}, f32[9,128,128]{2,1,0:T(8,128)S(1)}) custom-call(s32[8,2]{1,0:T(8,128)S(1)} %collective-permute-done.offsets.mid, f32[4,64,2048]{2,1,0:T(8,128)S(1)} %bitcast.11, f32[2,6,64,128]{3,2,1,0:T(8,128)S(1)} %collective-permute-done.2.above, ...), custom_call_target="tpu_custom_call" | custom-call | flops 4831838208 | bytes 8388608 | tf_op jit(solution)/shard_map/pallas_call | solution.py:270
  32.9 5.8 %collective-permute-done.5.below = f32[4,4,64,128]{3,2,1,0:T(8,128)S(1)} collective-permute-done((f32[4,4,64,128]{3,2,1,0:T(8,128)S(1)}, f32[4,4,64,128]{3,2,1,0:T(8,128)S(1)}, u32[]{:S(2)}, u32[]{:S(2)}) %collective-permute-start.5) | collective-permute-done | bytes 524320 | tf_op jit(solution)/shard_map/ppermute | solution.py:20
  38.7 0.0 collective-permute-done.4.above
  38.7 0.0 collective-permute-start.7
  38.7 2.5 %collective-permute-start.6 = (f32[2,6,64,128]{3,2,1,0:T(8,128)S(1)}, f32[2,6,64,128]{3,2,1,0:T(8,128)S(1)}, u32[]{:S(2)}, u32[]{:S(2)}) collective-permute-start(f32[2,6,64,128]{3,2,1,0:T(8,128)S(1)} %get-tuple-element.49), channel_id=1, source_target_pairs={{0,1},{1,2},{2,3},{3,4},{4,5},{5,6},{6,7},{7,8},{8,9},{9,10},{10,1... | collective-permute-start | bytes 1179656 | tf_op jit(solution)/shard_map/ppermute | solution.py:20
  41.2 20.0 %shard_map.89 = (f32[4,4,64,128]{3,2,1,0:T(8,128)S(1)}, f32[4,4,64,128]{3,2,1,0:T(8,128)S(1)}, f32[4,4,64,128]{3,2,1,0:T(8,128)S(1)}, f32[9,128,128]{2,1,0:T(8,128)S(1)}) custom-call(s32[8,2]{1,0:T(8,128)S(1)} %collective-permute-done.offsets.mid, f32[4,64,2048]{2,1,0:T(8,128)} %bitcast.7, f32[4,6,64,128]{3,2,1,0:T(8,128)S(1)} %collective-permute-done.4.above, ...), custom_call_target="tpu_custom_call" | custom-call | flops 9663676416 | bytes 8388608 | tf_op jit(solution)/shard_map/pallas_call | solution.py:270
  61.2 0.1 collective-permute-start.9
  61.3 1.7 %collective-permute-start.11 = (f32[4,4,64,128]{3,2,1,0:T(8,128)S(1)}, f32[4,4,64,128]{3,2,1,0:T(8,128)S(1)}, u32[]{:S(2)}, u32[]{:S(2)}) collective-permute-start(f32[4,4,64,128]{3,2,1,0:T(8,128)S(1)} %get-tuple-element.58), channel_id=1, source_target_pairs={{0,1},{1,2},{2,3},{3,4},{4,5},{5,6},{6,7},{7,8},{8,9},{9,10},{10,1... | collective-permute-start | bytes 1572872 | tf_op jit(solution)/shard_map/ppermute | solution.py:20
  63.0 0.0 collective-permute-start.8
  63.0 0.0 collective-permute-done.7.below
  63.0 1.7 %collective-permute-start.10 = (f32[2,4,64,128]{3,2,1,0:T(8,128)S(1)}, f32[2,4,64,128]{3,2,1,0:T(8,128)S(1)}, u32[]{:S(2)}, u32[]{:S(2)}) collective-permute-start(f32[2,4,64,128]{3,2,1,0:T(8,128)S(1)} %get-tuple-element.57), channel_id=1, source_target_pairs={{0,1},{1,2},{2,3},{3,4},{4,5},{5,6},{6,7},{7,8},{8,9},{9,10},{10,1... | collective-permute-start | bytes 786440 | tf_op jit(solution)/shard_map/ppermute | solution.py:20
  64.8 11.8 %shard_map.90 = (f32[2,4,64,128]{3,2,1,0:T(8,128)S(1)}, f32[2,4,64,128]{3,2,1,0:T(8,128)S(1)}, f32[2,4,64,128]{3,2,1,0:T(8,128)S(1)}, f32[9,128,128]{2,1,0:T(8,1...) custom-call(s32[8,2]{1,0:T(8,128)S(1)} %collective-permute-done.offsets.mid, f32[4,64,2048]{2,1,0:T(8,128)} %bitcast.8, ...), custom_call_target="tpu_custom_call" | custom-call | flops 4831838208 | bytes 8388608 | tf_op jit(solution)/shard_map/pallas_call | solution.py:270
  76.6 3.4 %collective-permute-done.8.refs_3_ = f32[2,4,64,128]{3,2,1,0:T(8,128)S(1)} collective-permute-done((f32[2,4,64,128]{3,2,1,0:T(8,128)S(1)}, f32[2,4,64,128]{3,2,1,0:T(8,128)S(1)}, u32[]{:S(2)}, u32[]{:S(2)}) %collective-permute-start.8) | collective-permute-done | bytes 262176 | tf_op jit(solution)/shard_map/ppermute | solution.py:20
  80.0 0.3 collective-permute-done.10.refs_6_
  80.2 0.0 collective-permute-done.9.refs_4_
  80.2 0.0 collective-permute-done.11.refs_7_
  80.2 0.0 collective-permute-start.12
  80.2 0.5 collective-permute-start.13
  80.7 2.1 %collective-permute-start.14 = (f32[2,4,64,128]{3,2,1,0:T(8,128)S(1)}, f32[2,4,64,128]{3,2,1,0:T(8,128)S(1)}, u32[]{:S(2)}, u32[]{:S(2)}) collective-permute-start(f32[2,4,64,128]{3,2,1,0:T(8,128)S(1)} %get-tuple-element.66), channel_id=1, source_target_pairs={{0,1},{1,2},{2,3},{3,4},{4,5},{5,6},{6,7},{7,8},{8,9},{9,10},{10,1... | collective-permute-start | bytes 786440 | tf_op jit(solution)/shard_map/ppermute | solution.py:20
  82.9 4.3 %collective-permute-done.13.refs_5_ = f32[2,4,64,128]{3,2,1,0:T(8,128)S(1)} collective-permute-done((f32[2,4,64,128]{3,2,1,0:T(8,128)S(1)}, f32[2,4,64,128]{3,2,1,0:T(8,128)S(1)}, u32[]{:S(2)}, u32[]{:S(2)}) %collective-permute-start.13) | collective-permute-done | bytes 262176 | tf_op jit(solution)/shard_map/ppermute | solution.py:20
  87.1 1.8 %collective-permute-done.14.refs_8_ = f32[2,4,64,128]{3,2,1,0:T(8,128)S(1)} collective-permute-done((f32[2,4,64,128]{3,2,1,0:T(8,128)S(1)}, f32[2,4,64,128]{3,2,1,0:T(8,128)S(1)}, u32[]{:S(2)}, u32[]{:S(2)}) %collective-permute-start.14) | collective-permute-done | bytes 262176 | tf_op jit(solution)/shard_map/ppermute | solution.py:20
  89.0 0.7 copy-done.3
  89.7 11.7 %all_to_all.10.parts = f32[8,9,8,128]{3,2,1,0:T(8,128)S(1)} all-to-all(f32[8,9,8,128]{3,2,1,0:T(8,128)S(1)} %add.3), channel_id=1, replica_groups={{0,2,4,6,8,10,12,14},{1,3,5,7,9,11,13,15},{16,18,20,22,24,26,28,30},{17..., dimensions={0} | all-to-all | bytes 589824 | tf_op jit(solution)/shard_map/all_to_all | solution.py:291
  101.3 0.9 shard_map.92
  102.2 7.0 %all-to-all-start.1 = ((f32[16,8,8,128]{3,2,1,0:T(8,128)}), f32[16,8,8,128]{3,2,1,0:T(8,128)S(1)}, u32[]{:S(2)}, u32[]{:S(2)}) async-start(f32[16,8,8,128]{3,2,1,0:T(8,128)} %shard_map.92), calls=%async_computation.1 | async-start | bytes 1048576 | tf_op jit(solution)/shard_map/all_to_all | solution.py:301
  109.2 0.9 copy-done.4
  110.2 5.5 %shard_map.91 = f32[4,64,2048]{2,1,0:T(8,128)} custom-call(s32[8,2]{1,0:T(8,128)S(1)} %copy.13.own, s32[8,2]{1,0:T(8,128)S(1)} %collective-permute-done.offsets.mid, s32[8,2]{1,0:T(8,128)S(1)} %collective-permute-done.1.far, f32[2,4,64,128]{3,2,1,0:T(8,128)S(1)} %get-tuple-element.40.refs_0_, f32[4,4,64,128]{3,2,1,0:T(8,128)S(1)} %get-tuple-element.46.refs_1_, ...), custom_call_target="tpu_custom_call" | custom-call | bytes 5242880 | tf_op jit(solution)/shard_map/pallas_call | solution.py:303
  115.7 7.7 %all-to-all-done.1.parts = f32[16,8,8,128]{3,2,1,0:T(8,128)S(1)} async-done(((f32[16,8,8,128]{3,2,1,0:T(8,128)}), f32[16,8,8,128]{3,2,1,0:T(8,128)S(1)}, u32[]{:S(2)}, u32[]{:S(2)}) %all-to-all-start.1) | async-done | bytes 524320 | tf_op jit(solution)/shard_map/all_to_all | solution.py:301
  123.4 0.8 shard_map.93
  (14 shorter events, 0.1 us)
Async XLA Ops:
  1.4 6.1 %collective-permute-start.1 = (s32[8,2]{1,0:T(8,128)S(1)}, s32[8,2]{1,0:T(8,128)S(1)}, u32[]{:S(2)}, u32[]{:S(2)}) collective-permute-start(s32[8,2]{1,0:T(8,128)S(1)} %copy.13.own), channel_id=1, source_target_pairs={{0,2},{1,3},{2,4},{3,5},{4,6},{5,7},{6,8},{7,9},{8,10},{9,11},{10,... | collective-permute-start | bytes 200 | tf_op jit(solution)/shard_map/ppermute | solution.py:20
  7.5 1.6 %copy-start = (f32[2,2,64,2048]{3,2,1,0:T(8,128)S(1)}, f32[2,2,64,2048]{3,2,1,0:T(8,128)}, u32[]{:S(2)}) copy-start(f32[2,2,64,2048]{3,2,1,0:T(8,128)} %param.7) | copy-start | bytes 6291460
  9.1 1.0 copy-start.2
  10.1 11.3 %copy-start.7 = (f32[128,128]{1,0:T(8,128)S(1)}, f32[128,128]{1,0:T(8,128)}, u32[]{:S(2)}) copy-start(f32[128,128]{1,0:T(8,128)} %param.9) | copy-start | bytes 196612
  11.1 11.9 %copy-start.1 = (f32[2,2,64,2048]{3,2,1,0:T(8,128)S(1)}, f32[2,2,64,2048]{3,2,1,0:T(8,128)}, u32[]{:S(2)}) copy-start(f32[2,2,64,2048]{3,2,1,0:T(8,128)} %param.7) | copy-start | bytes 6291460
  11.1 11.9 %copy-start.5 = (f32[4,2,128,128]{3,2,1,0:T(8,128)S(1)}, f32[4,2,128,128]{3,2,1,0:T(8,128)}, u32[]{:S(2)}) copy-start(f32[4,2,128,128]{3,2,1,0:T(8,128)} %probe.5) | copy-start | bytes 1572868
  11.2 11.9 %copy-start.6 = (bf16[4,256,256]{2,1,0:T(8,128)(2,1)S(1)}, bf16[4,256,256]{2,1,0:T(8,128)(2,1)}, u32[]{:S(2)}) copy-start(bf16[4,256,256]{2,1,0:T(8,128)(2,1)} %constant.4.clone.tables) | copy-start | bytes 1572868
  11.2 7.7 %collective-permute-start.2 = (f32[2,6,64,128]{3,2,1,0:T(8,128)S(1)}, f32[2,6,64,128]{3,2,1,0:T(8,128)S(1)}, u32[]{:S(2)}, u32[]{:S(2)}) collective-permute-start(f32[2,6,64,128]{3,2,1,0:T(8,128)S(1)} %get-tuple-element.38), channel_id=1, source_target_pairs={{0,1},{1,2},{2,3},{3,4},{4,5},{5,6},{6,7},{7,8},{8,9},{9,10},{10,1... | collective-permute-start | bytes 1179656 | tf_op jit(solution)/shard_map/ppermute | solution.py:20
  11.4 5.8 %collective-permute-start.3 = (f32[2,4,64,128]{3,2,1,0:T(8,128)S(1)}, f32[2,4,64,128]{3,2,1,0:T(8,128)S(1)}, u32[]{:S(2)}, u32[]{:S(2)}) collective-permute-start(f32[2,4,64,128]{3,2,1,0:T(8,128)S(1)} %get-tuple-element.39), channel_id=1, source_target_pairs={{0,15},{1,0},{2,1},{3,2},{4,3},{5,4},{6,5},{7,6},{8,7},{9,8},{10,9... | collective-permute-start | bytes 786440 | tf_op jit(solution)/shard_map/ppermute | solution.py:20
  12.8 10.1 %collective-permute-start = (s32[8,2]{1,0:T(8,128)S(1)}, s32[8,2]{1,0:T(8,128)S(1)}, u32[]{:S(2)}, u32[]{:S(2)}) collective-permute-start(s32[8,2]{1,0:T(8,128)S(1)} %copy.13.own), channel_id=1, source_target_pairs={{0,1},{1,2},{2,3},{3,4},{4,5},{5,6},{6,7},{7,8},{8,9},{9,10},{10,1... | collective-permute-start | bytes 200 | tf_op jit(solution)/shard_map/ppermute | solution.py:20
  18.9 19.8 %collective-permute-start.4 = (f32[4,6,64,128]{3,2,1,0:T(8,128)S(1)}, f32[4,6,64,128]{3,2,1,0:T(8,128)S(1)}, u32[]{:S(2)}, u32[]{:S(2)}) collective-permute-start(f32[4,6,64,128]{3,2,1,0:T(8,128)S(1)} %get-tuple-element.43), channel_id=1, source_target_pairs={{0,1},{1,2},{2,3},{3,4},{4,5},{5,6},{6,7},{7,8},{8,9},{9,10},{10,1... | collective-permute-start | bytes 2359304 | tf_op jit(solution)/shard_map/ppermute | solution.py:20
  21.6 17.1 %collective-permute-start.5 = (f32[4,4,64,128]{3,2,1,0:T(8,128)S(1)}, f32[4,4,64,128]{3,2,1,0:T(8,128)S(1)}, u32[]{:S(2)}, u32[]{:S(2)}) collective-permute-start(f32[4,4,64,128]{3,2,1,0:T(8,128)S(1)} %get-tuple-element.44), channel_id=1, source_target_pairs={{0,15},{1,0},{2,1},{3,2},{4,3},{5,4},{6,5},{7,6},{8,7},{9,8},{10,9... | collective-permute-start | bytes 1572872 | tf_op jit(solution)/shard_map/ppermute | solution.py:20
  38.7 24.3 %collective-permute-start.7 = (f32[2,4,64,128]{3,2,1,0:T(8,128)S(1)}, f32[2,4,64,128]{3,2,1,0:T(8,128)S(1)}, u32[]{:S(2)}, u32[]{:S(2)}) collective-permute-start(f32[2,4,64,128]{3,2,1,0:T(8,128)S(1)} %get-tuple-element.50), channel_id=1, source_target_pairs={{0,15},{1,0},{2,1},{3,2},{4,3},{5,4},{6,5},{7,6},{8,7},{9,8},{10,9... | collective-permute-start | bytes 786440 | tf_op jit(solution)/shard_map/ppermute | solution.py:20
  38.7 26.0 %collective-permute-start.6 = (f32[2,6,64,128]{3,2,1,0:T(8,128)S(1)}, f32[2,6,64,128]{3,2,1,0:T(8,128)S(1)}, u32[]{:S(2)}, u32[]{:S(2)}) collective-permute-start(f32[2,6,64,128]{3,2,1,0:T(8,128)S(1)} %get-tuple-element.49), channel_id=1, source_target_pairs={{0,1},{1,2},{2,3},{3,4},{4,5},{5,6},{6,7},{7,8},{8,9},{9,10},{10,1... | collective-permute-start | bytes 1179656 | tf_op jit(solution)/shard_map/ppermute | solution.py:20
  61.2 19.0 %collective-permute-start.9 = (f32[4,4,64,128]{3,2,1,0:T(8,128)S(1)}, f32[4,4,64,128]{3,2,1,0:T(8,128)S(1)}, u32[]{:S(2)}, u32[]{:S(2)}) collective-permute-start(f32[4,4,64,128]{3,2,1,0:T(8,128)S(1)} %get-tuple-element.56), channel_id=1, source_target_pairs={{0,15},{1,0},{2,1},{3,2},{4,3},{5,4},{6,5},{7,6},{8,7},{9,8},{10,9... | collective-permute-start | bytes 1572872 | tf_op jit(solution)/shard_map/ppermute | solution.py:20
  61.3 18.9 %collective-permute-start.11 = (f32[4,4,64,128]{3,2,1,0:T(8,128)S(1)}, f32[4,4,64,128]{3,2,1,0:T(8,128)S(1)}, u32[]{:S(2)}, u32[]{:S(2)}) collective-permute-start(f32[4,4,64,128]{3,2,1,0:T(8,128)S(1)} %get-tuple-element.58), channel_id=1, source_target_pairs={{0,1},{1,2},{2,3},{3,4},{4,5},{5,6},{6,7},{7,8},{8,9},{9,10},{10,1... | collective-permute-start | bytes 1572872 | tf_op jit(solution)/shard_map/ppermute | solution.py:20
  63.0 16.9 %collective-permute-start.8 = (f32[2,4,64,128]{3,2,1,0:T(8,128)S(1)}, f32[2,4,64,128]{3,2,1,0:T(8,128)S(1)}, u32[]{:S(2)}, u32[]{:S(2)}) collective-permute-start(f32[2,4,64,128]{3,2,1,0:T(8,128)S(1)} %get-tuple-element.55), channel_id=1, source_target_pairs={{0,15},{1,0},{2,1},{3,2},{4,3},{5,4},{6,5},{7,6},{8,7},{9,8},{10,9... | collective-permute-start | bytes 786440 | tf_op jit(solution)/shard_map/ppermute | solution.py:20
  63.0 17.2 %collective-permute-start.10 = (f32[2,4,64,128]{3,2,1,0:T(8,128)S(1)}, f32[2,4,64,128]{3,2,1,0:T(8,128)S(1)}, u32[]{:S(2)}, u32[]{:S(2)}) collective-permute-start(f32[2,4,64,128]{3,2,1,0:T(8,128)S(1)} %get-tuple-element.57), channel_id=1, source_target_pairs={{0,1},{1,2},{2,3},{3,4},{4,5},{5,6},{6,7},{7,8},{8,9},{9,10},{10,1... | collective-permute-start | bytes 786440 | tf_op jit(solution)/shard_map/ppermute | solution.py:20
  80.2 2.6 %collective-permute-start.12 = (f32[8,9,8,128]{3,2,1,0:T(8,128)S(1)}, f32[8,9,8,128]{3,2,1,0:T(8,128)S(1)}, u32[]{:S(2)}, u32[]{:S(2)}) collective-permute-start(f32[8,9,8,128]{3,2,1,0:T(8,128)S(1)} %get-tuple-element.60), channel_id=1, source_target_pairs={{0,1},{1,0},{2,3},{3,2},{4,5},{5,4},{6,7},{7,6},{8,9},{9,8},{10,11... | collective-permute-start | bytes 884744 | tf_op jit(solution)/shard_map/ppermute | solution.py:289
  80.2 6.9 %collective-permute-start.13 = (f32[2,4,64,128]{3,2,1,0:T(8,128)S(1)}, f32[2,4,64,128]{3,2,1,0:T(8,128)S(1)}, u32[]{:S(2)}, u32[]{:S(2)}) collective-permute-start(f32[2,4,64,128]{3,2,1,0:T(8,128)S(1)} %get-tuple-element.63), channel_id=1, source_target_pairs={{0,15},{1,0},{2,1},{3,2},{4,3},{5,4},{6,5},{7,6},{8,7},{9,8},{10,9... | collective-permute-start | bytes 786440 | tf_op jit(solution)/shard_map/ppermute | solution.py:20
  80.7 8.2 %collective-permute-start.14 = (f32[2,4,64,128]{3,2,1,0:T(8,128)S(1)}, f32[2,4,64,128]{3,2,1,0:T(8,128)S(1)}, u32[]{:S(2)}, u32[]{:S(2)}) collective-permute-start(f32[2,4,64,128]{3,2,1,0:T(8,128)S(1)} %get-tuple-element.66), channel_id=1, source_target_pairs={{0,1},{1,2},{2,3},{3,4},{4,5},{5,6},{6,7},{7,8},{8,9},{9,10},{10,1... | collective-permute-start | bytes 786440 | tf_op jit(solution)/shard_map/ppermute | solution.py:20
  89.0 0.7 copy-start.3
  102.2 21.2 %all-to-all-start.1 = ((f32[16,8,8,128]{3,2,1,0:T(8,128)}), f32[16,8,8,128]{3,2,1,0:T(8,128)S(1)}, u32[]{:S(2)}, u32[]{:S(2)}) async-start(f32[16,8,8,128]{3,2,1,0:T(8,128)} %shard_map.92), calls=%async_computation.1 | async-start | bytes 1048576 | tf_op jit(solution)/shard_map/all_to_all | solution.py:301
  109.2 0.9 copy-start.4
